TPU v7x, 256 devices: a whole 4x4x8 slice. The times are simulated.
256 devices in a mesh: expert: 32 (over z, y), dp: 8 (over x, core).
Axes of the slice: x: 4, y: 4, z: 8, core: 2. Of those that a mesh axis runs over, the one named last changes fastest.
Arguments:
- tokens: bfloat16 [65792, 1664], P(('expert', 'dp')), may hold values from -100 to 100
- upstream: bfloat16 [65792, 1664], P(('expert', 'dp')), may hold values from -6 to 6
- gate_values: float32 [65792, 2], P(('expert', 'dp')), may hold values from 0.2 to 1
- expert_index: int32 [65792, 2], P(('expert', 'dp')), may hold values from 0 to 31, as said below
- slot_index: int32 [65792, 2], P(('expert', 'dp')), may hold values from 0 to 3, as said below
- kept_mask: int32 [65792, 2], P(('expert', 'dp')), may hold values from 0 to 1, as said below
- counts: int32 [256, 32], P(('expert', 'dp')), may hold values from 0 to 4, as said below
- norm_gain: float32 [1664], replicated, may hold values from 0.1 to 1.9
- norm_bias: float32 [1664], replicated, may hold values from -3 to 3
- in_weight: bfloat16 [32, 1664, 4096], P('expert', None, 'dp'), may hold values from -0.15625 to 0.15625
- out_weight: bfloat16 [32, 4096, 1664], P('expert', 'dp'), may hold values from -0.09375 to 0.09375
Outputs:
- mixed_out: bfloat16 [65792, 1664], P(('expert', 'dp'))
- grad_in: bfloat16 [65792, 1664], P(('expert', 'dp'))
- grad_in_weight: bfloat16 [32, 1664, 4096], P('expert', None, 'dp')
- grad_out_weight: bfloat16 [32, 4096, 1664], P('expert', 'dp')
Inputs may be any that keep to these rules, and one draw needn't show every extreme that they name: `expert_index`: A token's two choices name different experts. Some expert is the first choice of the 5 highest-priority tokens of every device. `slot_index`: each device serves its choices in one priority order of its tokens, all first choices before any second choice; a kept choice's slot counts the earlier choices of that device for the same expert, so the kept slots of one device and expert are distinct and run from 0 upward. A dropped choice has slot 0. `kept_mask`: 1 exactly where the choice's rank for its expert on its device is under 4; every device drops some choice. `counts`: at most the number of kept choices of the device for the expert, and below it for some devices and experts.
All inputs are finite; a program needn't handle non-finite values.
Results may differ from a plain program's by a relative error of at most 0.0068.
Values may be sent and summed in bfloat16 or wider, within the bound.
No kernel may reach another device: no remote copies, remote signals or barrier semaphores. Data moves between devices by JAX's collectives and lax.ppermute only.
A program may use at most 128 MiB of HBM per device.

v0:
```python
import functools

import jax
import jax.numpy as jnp
from jax import lax
from jax.experimental import pallas as pl
from jax.experimental.pallas import tpu as pltpu
from jax.sharding import PartitionSpec as P

CAP = 4
EPSILON = 1e-06
HBM = pl.BlockSpec(memory_space=pltpu.HBM)
VMEM = pl.BlockSpec(memory_space=pltpu.VMEM)
MIB = 1024 * 1024
F32 = jnp.float32
BF16 = jnp.bfloat16
TN = (((0,), (0,)), ((), ()))
NT = (((1,), (1,)), ((), ()))
sds = jax.ShapeDtypeStruct


def call(body, outs, ins, scalars=(), here=(), keep=(), flops=0, name=None):
    n_in, n_out, n_s = len(ins), len(outs), len(scalars)
    far_in = [i for i in range(n_in) if i not in here]
    far_out = [i for i in range(n_out) if i not in keep]

    def kernel(*refs):
        words, refs = refs[:n_s], refs[n_s:]
        source, refs = refs[:n_in], refs[n_in:]
        sink, refs = refs[:n_out], refs[n_out:]
        held, refs = dict(zip(far_in, refs)), refs[len(far_in) :]
        made, refs = dict(zip(far_out, refs)), refs[len(far_out) :]
        in_sem, out_sem, word_sem, *smem = refs
        word_copies = [pltpu.make_async_copy(a, b, word_sem.at[k]) for k, (a, b) in enumerate(zip(words, smem))]
        for c in word_copies:
            c.start()
        copies = {i: pltpu.make_async_copy(source[i], held[i], in_sem.at[k]) for k, i in enumerate(far_in)}
        for c in copies.values():
            c.start()
        for c in word_copies:
            c.wait()
        waited, sent = set(), []

        def load(i):
            if i not in copies:
                return source[i]
            if i not in waited:
                waited.add(i)
                copies[i].wait()
            return held[i]

        def store(i):
            if i in made:
                c = pltpu.make_async_copy(made[i], sink[i], out_sem.at[far_out.index(i)])
                c.start()
                sent.append(c)

        body(load, [made.get(i, sink[i]) for i in range(n_out)], store, smem)
        for c in sent:
            c.wait()

    moved = sum(a.size * a.dtype.itemsize for a in list(outs) + list(ins))
    buffers = [pltpu.VMEM(ins[i].shape, ins[i].dtype) for i in far_in]
    buffers += [pltpu.VMEM(outs[i].shape, outs[i].dtype) for i in far_out]
    sems = [pltpu.SemaphoreType.DMA((max(1, len(k)),)) for k in (far_in, far_out, scalars)]
    words = [pltpu.SMEM(a.shape, a.dtype) for a in scalars]
    scalars = [pltpu.with_memory_space_constraint(a, pltpu.HBM) for a in scalars]
    ins = [a if i in here else pltpu.with_memory_space_constraint(a, pltpu.HBM) for i, a in enumerate(ins)]
    outs = [o if i in keep else pltpu.HBM(o.shape, o.dtype) for i, o in enumerate(outs)]
    return pl.pallas_call(
        kernel,
        out_shape=outs,
        in_specs=[HBM] * n_s + [VMEM if i in here else HBM for i in range(n_in)],
        out_specs=[VMEM if i in keep else HBM for i in range(n_out)],
        scratch_shapes=buffers + sems + words,
        compiler_params=pltpu.CompilerParams(vmem_limit_bytes=36 * MIB),
        cost_estimate=pl.CostEstimate(flops=flops, bytes_accessed=moved, transcendentals=0),
        name=name,
    )(*scalars, *ins)


def after(values, *others):
    return lax.optimization_barrier((values, others))[0]


def standardize(floats):
    center = jnp.mean(floats, axis=-1, keepdims=True)
    spread = jnp.mean(jnp.square(floats - center), axis=-1, keepdims=True)
    inv_std = lax.rsqrt(spread + EPSILON)
    return (floats - center) * inv_std, inv_std


def one_hots(target, slots):
    rows = lax.broadcasted_iota(jnp.int32, (slots, target.shape[1]), 0)
    return rows == target[0:1], rows == target[1:2]


def either(first, second):
    return jnp.where(first | second, 1.0, 0.0).astype(BF16)


def weighted(first, second, gates):
    return jnp.where(first, gates[0:1], 0.0) + jnp.where(second, gates[1:2], 0.0)


def rows_of(ref, part):
    return ref[:, part].reshape(ref.shape[0] * ref.shape[2], ref.shape[3])


def dispatch(load, made, store, smem):
    (counts,) = smem
    experts = counts.shape[1]
    slots = experts * CAP
    chosen, slot, kept = load(0)[...], load(1)[...], load(2)[...]
    allowed = jnp.zeros(chosen.shape, jnp.int32)
    for e in range(experts):
        allowed = jnp.where(chosen == e, counts[0, e], allowed)
    active = (kept == 1) & (slot < allowed)
    target = jnp.where(active, chosen * CAP + slot, slots)
    made[1][...] = target
    store(1)
    first, second = one_hots(target, slots)
    pick = either(first, second)
    gate = jnp.sum(weighted(first, second, load(3)[...]), axis=1, keepdims=True)
    block = (experts, CAP, made[0].shape[3])
    rows = gate * jnp.dot(pick, load(4)[...], preferred_element_type=F32)
    made[0][:, 1] = rows.astype(BF16).reshape(block)
    standard, _ = standardize(load(5)[...].astype(F32))
    normed = (standard * load(6)[...][None] + load(7)[...][None]).astype(BF16)
    rows = jnp.dot(pick, normed, preferred_element_type=F32)
    made[0][:, 0] = rows.astype(BF16).reshape(block)
    store(0)


def expert_rows(n, load, made, store, smem):
    x_all, g_all = made[0], made[1]
    for part, out in ((0, x_all), (1, g_all)):
        at = 0
        for i in range(n):
            rows = rows_of(load(i), part)
            out[pl.ds(at, rows.shape[0]), :] = rows
            at += rows.shape[0]
        store(part)
    c = 0.7978845608028654
    out, back = None, None
    for k in range(2):
        w_in, w_out = load(n + 2 * k), load(n + 2 * k + 1)
        v = jnp.dot(x_all[...], w_in[...], preferred_element_type=F32)
        square = v * v
        t = jnp.tanh(c * v * (1.0 + 0.044715 * square))
        act, grad = made[2 + k], made[4 + k]
        act[...] = (0.5 * v * (1.0 + t)).astype(BF16)
        store(2 + k)
        slope = 0.5 * (1.0 + t) + 0.5 * v * (1.0 - t * t) * (c * (1.0 + 3 * 0.044715 * square))
        hidden = lax.dot_general(g_all[...], w_out[...], NT, preferred_element_type=F32)
        grad[...] = (hidden * slope).astype(BF16)
        store(4 + k)
        term = jnp.dot(act[...], w_out[...], preferred_element_type=F32)
        out = term if out is None else out + term
        term = lax.dot_general(grad[...], w_in[...], NT, preferred_element_type=F32)
        back = term if back is None else back + term
    at = 0
    for i in range(6, len(made)):
        ref = made[i]
        size = ref.shape[0] * CAP
        for part, total in ((0, out), (1, back)):
            piece = total[at : at + size].astype(ref.dtype)
            ref[:, part] = piece.reshape(ref.shape[0], CAP, ref.shape[3])
        store(i)
        at += size


def tall_product(load, first):
    total = None
    for i in (first, first + 2, first + 4):
        term = lax.dot_general(load(i)[...], load(i + 1)[...], TN, preferred_element_type=F32)
        total = term if total is None else total + term
    return total


def weight_grads(load, made, store, smem):
    for k in range(2):
        made[k][...] = tall_product(load, 6 * k).astype(BF16)
        store(k)


def weight_sums(load, made, store, smem):
    for k in range(2):
        made[k][...] = (tall_product(load, 6 * k) + load(12 + k)[...].astype(F32)).astype(BF16)
        store(k)


def home_sum(load, made, store, smem):
    half = made[0].shape[0] // 2
    for k in range(2):
        part = pl.ds(k * half, half)
        total = load(0)[part] + load(1 + k)[...].astype(F32) + load(3 + k)[...].astype(F32)
        made[0][part] = total.astype(BF16)
    store(0)


def combine(load, made, store, smem):
    target, gates = load(0)[...], load(1)[...]
    tokens = load(2)[...].astype(F32)
    standard, inv_std = standardize(tokens)
    home = load(5)
    first, second = one_hots(target, home.shape[0] * CAP)
    rows = rows_of(home, 0)
    weight = weighted(first, second, gates)
    total = tokens
    for _ in range(3):
        part = weight.astype(BF16)
        weight = weight - part.astype(F32)
        total = total + lax.dot_general(part, rows, TN, preferred_element_type=F32)
    made[0][...] = total.astype(BF16)
    store(0)
    back = lax.dot_general(either(first, second), rows_of(home, 1), TN, preferred_element_type=F32)
    scaled = back * load(3)[...][None]
    inner = jnp.mean(scaled * standard, axis=-1, keepdims=True)
    centred = scaled - jnp.mean(scaled, axis=-1, keepdims=True) - standard * inner
    made[1][...] = (load(4)[...].astype(F32) + inv_std * centred).astype(BF16)
    store(1)


def on_device(n_dp, tokens, upstream, gates, expert, slot, kept, counts, gain, bias, in_weight, out_weight):
    experts = counts.shape[1]
    slots = experts * CAP
    n_tok, features = tokens.shape
    in_a, out_a = in_weight[0], out_weight[0]
    hidden = in_a.shape[1]
    half = experts // 2
    n_rows = slots * n_dp // 2
    right = [(i, (i + 2) % n_dp) for i in range(n_dp)]
    left = [(i, (i - 2) % n_dp) for i in range(n_dp)]
    sibling = [(i, i ^ 1) for i in range(n_dp)]

    def send(array, pairs):
        return lax.ppermute(array, "dp", pairs)

    def exchange(rows):
        return lax.all_to_all(rows, "expert", 0, 0, tiled=True)

    def add(a, b):
        return (a.astype(F32) + b.astype(F32)).astype(BF16)

    gates_t, expert_t, slot_t, kept_t = gates.T, expert.T, slot.T, kept.T
    block = sds((experts, 2, CAP, features), BF16)
    half_block = sds((half, 2, CAP, features), BF16)
    small = 2 * slots * n_tok * features
    in_b, out_b = send(in_a, sibling), send(out_a, sibling)
    rows, target = call(
        dispatch,
        [block, sds((2, n_tok), jnp.int32)],
        [expert_t, slot_t, kept_t, gates_t, upstream, tokens, gain, bias],
        scalars=[counts],
        keep=[0],
        flops=2 * small,
        name="dispatch",
    )
    rows, in_b, out_b = lax.optimization_barrier((exchange(rows), in_b, out_b))
    from_right, from_left = send(rows, left), send(rows, right)

    def experts_of(blocks, results, name):
        n = sum(b.shape[0] for b in blocks) * CAP
        wide, narrow = sds((n, features), BF16), sds((n, hidden), BF16)
        return call(
            functools.partial(expert_rows, len(blocks)),
            [wide, wide] + [narrow] * 4 + results,
            [*blocks, in_a, out_a, in_b, out_b],
            here=range(len(blocks) + 4),
            keep=range(6, 6 + len(results)),
            flops=16 * n * features * hidden,
            name=name,
        )

    own_block = sds(block.shape, F32)
    x_own, g_own, own_act_a, own_act_b, own_grad_a, own_grad_b, own = experts_of([rows], [own_block], "own_rows")
    from_right, from_left, own = lax.optimization_barrier((from_right, from_left, own))
    far_top, far_bottom = send(from_right[:half], left), send(from_left[half:], right)
    x_near, g_near, act_a, act_b, grad_a, grad_b, right_top, right_bottom, left_top, left_bottom = experts_of(
        [from_right, from_left], [half_block] * 4, "near_rows"
    )
    far_top, far_bottom, right_bottom, left_top = lax.optimization_barrier(
        (far_top, far_bottom, right_bottom, left_top)
    )
    right_bottom, left_top = send(right_bottom, right), send(left_top, left)
    x_far, g_far, far_act_a, far_act_b, far_grad_a, far_grad_b, far_top, far_bottom = experts_of(
        [far_top, far_bottom], [half_block] * 2, "far_rows"
    )
    far_top, far_bottom = send(far_top, right), send(far_bottom, left)
    first, second = sds(in_a.shape, BF16), sds(out_a.shape, BF16)
    flops = 4 * n_rows * features * hidden
    first_b, second_b = call(
        weight_grads,
        [first, second],
        after([x_near, grad_b], right_bottom, left_top)
        + [x_far, far_grad_b, x_own, own_grad_b, act_b, g_near, far_act_b, g_far, own_act_b, g_own],
        keep=range(2),
        flops=flops,
        name="weights_b",
    )
    right_top, left_bottom, first_b, second_b = lax.optimization_barrier(
        (add(right_top, far_top), add(left_bottom, far_bottom), first_b, second_b)
    )
    right_top, left_bottom = send(right_top, right), send(left_bottom, left)
    more_first, more_second = send(first_b, sibling), send(second_b, sibling)
    parts = [own, right_top, right_bottom, left_top, left_bottom]
    (home,) = call(home_sum, [block], parts, here=range(5), keep=[0], name="home_sum")
    home = exchange(home)
    grad_first, grad_second = call(
        weight_sums,
        [first, second],
        [x_near, grad_a, x_far, far_grad_a, x_own, own_grad_a]
        + [act_a, g_near, far_act_a, g_far, own_act_a, g_own, more_first, more_second],
        here=(12, 13),
        flops=flops,
        name="weights_a",
    )
    home = after(home, grad_first)
    like = sds(tokens.shape, BF16)
    mixed, grad_in = call(
        combine,
        [like, like],
        [target, gates_t, tokens, gain, upstream, home],
        here=[5],
        flops=4 * small,
        name="combine",
    )
    return mixed, grad_in, grad_first[None], grad_second[None]


def solution(mesh):
    rows = P(("expert", "dp"), None)
    in_specs = (rows,) * 7 + (P(), P(), P("expert", None, "dp"), P("expert", "dp", None))
    out_specs = (rows, rows, P("expert", None, "dp"), P("expert", "dp", None))
    body = functools.partial(on_device, mesh.shape["dp"])
    return jax.shard_map(body, mesh=mesh, in_specs=in_specs, out_specs=out_specs, check_vma=False)
```

profile of v0, /device:TPU:8, one launch (start us, length us, event | category | flops | bytes accessed | tf_op | source)
XLA Modules:
  0.0 136.0 jit_solution(2028773069312866055)
XLA Ops:
  0.7 0.5 collective-permute-start.1
  1.2 2.9 %dispatch.1 = (bf16[32,2,4,1664]{3,2,1,0:T(4,128)(2,1)S(1)}, s32[2,257]{1,0:T(2,128)}) custom-call(s32[1,32]{1,0:T(1,128)} %refs_0_.1, s32[2,257]{1,0:T(2,128)} %bitcast.18, s32[2,257]{1,0:T(2,128)} %bitcast.19, s32[2,257]{1,0:T(2,128)} %bitcast.20, f32[2,257]{1,0:T(2,128)} %bitcast.16, bf16[257,1664]{1,0:T(8,128)(2,1)} %refs_4_.1, ...), custom_call_target="tpu_custom_call" | custom-call | flops 218955776 | bytes 2586152 | tf_op jit(solution)/shard_map/dispatch/pallas_call | solution.py:70
  4.2 35.6 %all_to_all.10.refs_0_ = bf16[32,2,4,1664]{3,2,1,0:T(4,128)(2,1)S(1)} all-to-all(bf16[32,2,4,1664]{3,2,1,0:T(4,128)(2,1)S(1)} %get-tuple-element.55), channel_id=1, replica_groups=mesh['expert'=32,'dp'=8] {'expert'}, dimensions={0} | all-to-all | bytes 1703936 | tf_op jit(solution)/shard_map/all_to_all | solution.py:241
  39.8 1.5 %collective-permute-start.3 = (bf16[32,2,4,1664]{3,2,1,0:T(4,128)(2,1)S(1)}, bf16[32,2,4,1664]{3,2,1,0:T(4,128)(2,1)S(1)}, u32[]{:S(2)}, u32[]{:S(2)}) collective-permute-start(bf16[32,2,4,1664]{3,2,1,0:T(4,128)(2,1)S(1)} %all_to_all.10.refs_0_), channel_id=1, source_target_pairs={{0,2},{1,3},{2,4},{3,5},{4,6},{5,7},{6,0},{7,1},{8,10},{9,11},{10,... | collective-permute-start | bytes 2555912 | tf_op jit(solution)/shard_map/ppermute | solution.py:238
  41.3 1.7 %collective-permute-start.2 = (bf16[32,2,4,1664]{3,2,1,0:T(4,128)(2,1)S(1)}, bf16[32,2,4,1664]{3,2,1,0:T(4,128)(2,1)S(1)}, u32[]{:S(2)}, u32[]{:S(2)}) collective-permute-start(bf16[32,2,4,1664]{3,2,1,0:T(4,128)(2,1)S(1)} %all_to_all.10.refs_0_), channel_id=1, source_target_pairs={{0,6},{1,7},{2,0},{3,1},{4,2},{5,3},{6,4},{7,5},{8,14},{9,15},{10,... | collective-permute-start | bytes 2555912 | tf_op jit(solution)/shard_map/ppermute | solution.py:238
  43.1 3.1 %own_rows.1 = (bf16[128,1664]{1,0:T(8,128)(2,1)}, bf16[128,1664]{1,0:T(8,128)(2,1)}, bf16[128,512]{1,0:T(8,128)(2,1)}, bf16[128,512]{1,0:T(8,128)(2,1)}, bf16[12...) custom-call(bf16[32,2,4,1664]{3,2,1,0:T(4,128)(2,1)S(1)} %all_to_all.10.refs_0_, ...), custom_call_target="tpu_custom_call" | custom-call | flops 1744830464 | bytes 10747904 | tf_op jit(solution)/shard_map/own_rows/pallas_call | solution.py:70
  46.2 14.0 %collective-permute-done.3.refs_1_ = bf16[32,2,4,1664]{3,2,1,0:T(4,128)(2,1)S(1)} collective-permute-done((bf16[32,2,4,1664]{3,2,1,0:T(4,128)(2,1)S(1)}, bf16[32,2,4,1664]{3,2,1,0:T(4,128)(2,1)S(1)}, u32[]{:S(2)}, u32[]{:S(2)}) %collective-permute-start.3) | collective-permute-done | bytes 852000 | tf_op jit(solution)/shard_map/ppermute | solution.py:238
  60.4 0.1 slice.7
  60.5 1.6 %collective-permute-start.5 = (bf16[16,2,4,1664]{3,2,1,0:T(4,128)(2,1)S(1)}, bf16[16,2,4,1664]{3,2,1,0:T(4,128)(2,1)S(1)}, u32[]{:S(2)}, u32[]{:S(2)}) collective-permute-start(bf16[16,2,4,1664]{3,2,1,0:T(4,128)(2,1)S(1)} %slice.7), channel_id=1, source_target_pairs={{0,2},{1,3},{2,4},{3,5},{4,6},{5,7},{6,0},{7,1},{8,10},{9,11},{10,... | collective-permute-start | bytes 1277960 | tf_op jit(solution)/shard_map/ppermute | solution.py:238
  62.1 1.8 %collective-permute-start.4 = (bf16[16,2,4,1664]{3,2,1,0:T(4,128)(2,1)S(1)}, bf16[16,2,4,1664]{3,2,1,0:T(4,128)(2,1)S(1)}, u32[]{:S(2)}, u32[]{:S(2)}) collective-permute-start(bf16[16,2,4,1664]{3,2,1,0:T(4,128)(2,1)S(1)} %slice.6), channel_id=1, source_target_pairs={{0,6},{1,7},{2,0},{3,1},{4,2},{5,3},{6,4},{7,5},{8,14},{9,15},{10,... | collective-permute-start | bytes 1277960 | tf_op jit(solution)/shard_map/ppermute | solution.py:238
  63.8 4.9 %near_rows.1 = (bf16[256,1664]{1,0:T(8,128)(2,1)}, bf16[256,1664]{1,0:T(8,128)(2,1)}, bf16[256,512]{1,0:T(8,128)(2,1)}, bf16[256,512]{1,0:T(8,128)(2,1)}, bf16[2...) custom-call(bf16[32,2,4,1664]{3,2,1,0:T(4,128)(2,1)S(1)} %collective, ...), custom_call_target="tpu_custom_call" | custom-call | flops 3489660928 | bytes 12976128 | tf_op jit(solution)/shard_map/near_rows/pallas_call | solution.py:70
  68.7 2.2 %collective-permute-done.5.refs_1_ = bf16[16,2,4,1664]{3,2,1,0:T(4,128)(2,1)S(1)} collective-permute-done((bf16[16,2,4,1664]{3,2,1,0:T(4,128)(2,1)S(1)}, bf16[16,2,4,1664]{3,2,1,0:T(4,128)(2,1)S(1)}, u32[]{:S(2)}, u32[]{:S(2)}) %collective-permute-start.5) | collective-permute-done | bytes 426016 | tf_op jit(solution)/shard_map/ppermute | solution.py:238
  70.9 0.3 collective-permute-done.4.refs_0_
  71.2 0.7 collective-permute-start.8
  71.8 2.6 %collective-permute-start.9 = (bf16[16,2,4,1664]{3,2,1,0:T(4,128)(2,1)S(1)}, bf16[16,2,4,1664]{3,2,1,0:T(4,128)(2,1)S(1)}, u32[]{:S(2)}, u32[]{:S(2)}) collective-permute-start(bf16[16,2,4,1664]{3,2,1,0:T(4,128)(2,1)S(1)} %get-tuple-element.74), channel_id=1, source_target_pairs={{0,6},{1,7},{2,0},{3,1},{4,2},{5,3},{6,4},{7,5},{8,14},{9,15},{10,... | collective-permute-start | bytes 1277960 | tf_op jit(solution)/shard_map/ppermute | solution.py:238
  74.4 4.0 %far_rows.1 = (bf16[128,1664]{1,0:T(8,128)(2,1)}, bf16[128,1664]{1,0:T(8,128)(2,1)}, bf16[128,512]{1,0:T(8,128)(2,1)}, bf16[128,512]{1,0:T(8,128)(2,1)}, bf16[12...) custom-call(bf16[16,2,4,1664]{3,2,1,0:T(4,128)(2,1)S(1)} %collective, ...), custom_call_target="tpu_custom_call" | custom-call | flops 1744830464 | bytes 9895936 | tf_op jit(solution)/shard_map/far_rows/pallas_call | solution.py:70
  78.5 3.2 %collective-permute-start.7 = (bf16[16,2,4,1664]{3,2,1,0:T(4,128)(2,1)S(1)}, bf16[16,2,4,1664]{3,2,1,0:T(4,128)(2,1)S(1)}, u32[]{:S(2)}, u32[]{:S(2)}) collective-permute-start(bf16[16,2,4,1664]{3,2,1,0:T(4,128)(2,1)S(1)} %get-tuple-element.70), channel_id=1, source_target_pairs={{0,6},{1,7},{2,0},{3,1},{4,2},{5,3},{6,4},{7,5},{8,14},{9,15},{10,... | collective-permute-start | bytes 1277960 | tf_op jit(solution)/shard_map/ppermute | solution.py:238
  81.7 1.2 collective-permute-done.8.refs_2_
  83.0 6.3 %weights_b.1 = (bf16[1664,512]{1,0:T(8,128)(2,1)}, bf16[512,1664]{1,0:T(8,128)(2,1)}) custom-call(bf16[256,1664]{1,0:T(8,128)(2,1)} %get-tuple-element.75.refs_0_, bf16[256,512]{1,0:T(8,128)(2,1)} %get-tuple-element.76.refs_1_, bf16[128,1664]{1,0:T(8,128)(2,1)} %get-tuple-element.77.refs_2_, bf16[128,512]{1,0:T(8,128)(2,1)} %get-tuple-element.78.refs_3_, ...), custom_call_target="tpu_custom_call" | custom-call | flops 1744830464 | bytes 7864320 | tf_op jit(solution)/shard_map/weights_b/pallas_call | solution.py:70
  89.3 0.3 collective-permute-done.6
  89.6 0.2 add_convert_fusion.1
  89.9 0.2 add_convert_fusion
  90.1 2.5 %collective-permute-start.10 = (bf16[16,2,4,1664]{3,2,1,0:T(4,128)(2,1)S(1)}, bf16[16,2,4,1664]{3,2,1,0:T(4,128)(2,1)S(1)}, u32[]{:S(2)}, u32[]{:S(2)}) collective-permute-start(bf16[16,2,4,1664]{3,2,1,0:T(4,128)(2,1)S(1)} %add_convert_fusion.1), channel_id=1, source_target_pairs={{0,2},{1,3},{2,4},{3,5},{4,6},{5,7},{6,0},{7,1},{8,10},{9,11},{10,... | collective-permute-start | bytes 1277960 | tf_op jit(solution)/shard_map/ppermute | solution.py:238
  92.6 0.8 collective-permute-start.11
  93.5 0.5 collective-permute-start.13
  94.0 6.4 %collective-permute-done.10.refs_1_ = bf16[16,2,4,1664]{3,2,1,0:T(4,128)(2,1)S(1)} collective-permute-done((bf16[16,2,4,1664]{3,2,1,0:T(4,128)(2,1)S(1)}, bf16[16,2,4,1664]{3,2,1,0:T(4,128)(2,1)S(1)}, u32[]{:S(2)}, u32[]{:S(2)}) %collective-permute-start.10) | collective-permute-done | bytes 426016 | tf_op jit(solution)/shard_map/ppermute | solution.py:238
  100.4 0.3 collective-permute-done.11.refs_4_
  100.7 1.4 %home_sum.1 = bf16[32,2,4,1664]{3,2,1,0:T(4,128)(2,1)} custom-call(f32[32,2,4,1664]{3,2,1,0:T(4,128)S(1)} %get-tuple-element.60.refs_0_, bf16[16,2,4,1664]{3,2,1,0:T(4,128)(2,1)S(1)} %collective-permute-done.10.refs_1_, bf16[16,2,4,1664]{3,2,1,0:T(4,128)(2,1)S(1)} %collective-permute-done.8.refs_2_, ...), custom_call_target="tpu_custom_call" | custom-call | bytes 4259840 | tf_op jit(solution)/shard_map/home_sum/pallas_call | solution.py:70
  102.1 8.4 %all-to-all-start.1 = ((bf16[32,2,4,1664]{3,2,1,0:T(4,128)(2,1)}), bf16[32,2,4,1664]{3,2,1,0:T(4,128)(2,1)S(1)}, u32[]{:S(2)}, u32[]{:S(2)}) async-start(bf16[32,2,4,1664]{3,2,1,0:T(4,128)(2,1)} %home_sum.1), calls=%async_computation.1 | async-start | bytes 1703936 | tf_op jit(solution)/shard_map/all_to_all | solution.py:241
  110.5 7.8 %weights_a.1 = (bf16[1664,512]{1,0:T(8,128)(2,1)}, bf16[512,1664]{1,0:T(8,128)(2,1)}) custom-call(bf16[256,1664]{1,0:T(8,128)(2,1)} %get-tuple-element.75.refs_0_, bf16[256,512]{1,0:T(8,128)(2,1)} %get-tuple-element.91.refs_1_, bf16[128,1664]{1,0:T(8,128)(2,1)} %get-tuple-element.77.refs_2_, bf16[128,512]{1,0:T(8,128)(2,1)} %get-tuple-element.92.refs_3_, ...), custom_call_target="tpu_custom_call" | custom-call | flops 1744830464 | bytes 11272192 | tf_op jit(solution)/shard_map/weights_a/pallas_call | solution.py:70
  118.3 13.1 %all-to-all-done.1.refs_5_ = bf16[32,2,4,1664]{3,2,1,0:T(4,128)(2,1)S(1)} async-done(((bf16[32,2,4,1664]{3,2,1,0:T(4,128)(2,1)}), bf16[32,2,4,1664]{3,2,1,0:T(4,128)(2,1)S(1)}, u32[]{:S(2)}, u32[]{:S(2)}) %all-to-all-start.1) | async-done | bytes 852000 | tf_op jit(solution)/shard_map/all_to_all | solution.py:241
  131.4 4.4 %combine.1 = (bf16[257,1664]{1,0:T(8,128)(2,1)}, bf16[257,1664]{1,0:T(8,128)(2,1)}) custom-call(s32[2,257]{1,0:T(2,128)} %get-tuple-element.54.refs_0_, f32[2,257]{1,0:T(2,128)} %bitcast.17, bf16[257,1664]{1,0:T(8,128)(2,1)} %refs_2_.1, f32[1664]{0:T(1024)} %refs_3_.1, bf16[257,1664]{1,0:T(8,128)(2,1)} %refs_4_.1, ...), custom_call_target="tpu_custom_call" | custom-call | flops 437911552 | bytes 4283920 | tf_op jit(solution)/shard_map/combine/pallas_call | solution.py:70
  (15 shorter events, 0.4 us)
Async XLA Ops:
  0.6 39.2 %collective-permute-start = (bf16[1664,512]{1,0:T(8,128)(2,1)}, bf16[1664,512]{1,0:T(8,128)(2,1)S(1)}, u32[]{:S(2)}, u32[]{:S(2)}) collective-permute-start(bf16[1664,512]{1,0:T(8,128)(2,1)} %bitcast.8), channel_id=1, source_target_pairs={{0,1},{1,0},{2,3},{3,2},{4,5},{5,4},{6,7},{7,6},{8,9},{9,8},{10,11... | collective-permute-start | bytes 5111816 | tf_op jit(solution)/shard_map/ppermute | solution.py:238
  0.7 39.1 %collective-permute-start.1 = (bf16[512,1664]{1,0:T(8,128)(2,1)}, bf16[512,1664]{1,0:T(8,128)(2,1)S(1)}, u32[]{:S(2)}, u32[]{:S(2)}) collective-permute-start(bf16[512,1664]{1,0:T(8,128)(2,1)} %bitcast.12), channel_id=1, source_target_pairs={{0,1},{1,0},{2,3},{3,2},{4,5},{5,4},{6,7},{7,6},{8,9},{9,8},{10,11... | collective-permute-start | bytes 5111816 | tf_op jit(solution)/shard_map/ppermute | solution.py:238
  1.2 41.8 %copy-start = (bf16[1,1664,512]{2,1,0:T(8,128)(2,1)S(1)}, bf16[1,1664,512]{2,1,0:T(8,128)(2,1)}, u32[]{:S(2)}) copy-start(bf16[1,1664,512]{2,1,0:T(8,128)(2,1)} %param.20) | copy-start | bytes 5111812
  1.2 41.8 %copy-start.1 = (bf16[1,512,1664]{2,1,0:T(8,128)(2,1)S(1)}, bf16[1,512,1664]{2,1,0:T(8,128)(2,1)}, u32[]{:S(2)}) copy-start(bf16[1,512,1664]{2,1,0:T(8,128)(2,1)} %param.21) | copy-start | bytes 5111812
  39.8 20.4 %collective-permute-start.3 = (bf16[32,2,4,1664]{3,2,1,0:T(4,128)(2,1)S(1)}, bf16[32,2,4,1664]{3,2,1,0:T(4,128)(2,1)S(1)}, u32[]{:S(2)}, u32[]{:S(2)}) collective-permute-start(bf16[32,2,4,1664]{3,2,1,0:T(4,128)(2,1)S(1)} %all_to_all.10.refs_0_), channel_id=1, source_target_pairs={{0,2},{1,3},{2,4},{3,5},{4,6},{5,7},{6,0},{7,1},{8,10},{9,11},{10,... | collective-permute-start | bytes 2555912 | tf_op jit(solution)/shard_map/ppermute | solution.py:238
  41.3 18.9 %collective-permute-start.2 = (bf16[32,2,4,1664]{3,2,1,0:T(4,128)(2,1)S(1)}, bf16[32,2,4,1664]{3,2,1,0:T(4,128)(2,1)S(1)}, u32[]{:S(2)}, u32[]{:S(2)}) collective-permute-start(bf16[32,2,4,1664]{3,2,1,0:T(4,128)(2,1)S(1)} %all_to_all.10.refs_0_), channel_id=1, source_target_pairs={{0,6},{1,7},{2,0},{3,1},{4,2},{5,3},{6,4},{7,5},{8,14},{9,15},{10,... | collective-permute-start | bytes 2555912 | tf_op jit(solution)/shard_map/ppermute | solution.py:238
  60.5 10.4 %collective-permute-start.5 = (bf16[16,2,4,1664]{3,2,1,0:T(4,128)(2,1)S(1)}, bf16[16,2,4,1664]{3,2,1,0:T(4,128)(2,1)S(1)}, u32[]{:S(2)}, u32[]{:S(2)}) collective-permute-start(bf16[16,2,4,1664]{3,2,1,0:T(4,128)(2,1)S(1)} %slice.7), channel_id=1, source_target_pairs={{0,2},{1,3},{2,4},{3,5},{4,6},{5,7},{6,0},{7,1},{8,10},{9,11},{10,... | collective-permute-start | bytes 1277960 | tf_op jit(solution)/shard_map/ppermute | solution.py:238
  62.1 9.1 %collective-permute-start.4 = (bf16[16,2,4,1664]{3,2,1,0:T(4,128)(2,1)S(1)}, bf16[16,2,4,1664]{3,2,1,0:T(4,128)(2,1)S(1)}, u32[]{:S(2)}, u32[]{:S(2)}) collective-permute-start(bf16[16,2,4,1664]{3,2,1,0:T(4,128)(2,1)S(1)} %slice.6), channel_id=1, source_target_pairs={{0,6},{1,7},{2,0},{3,1},{4,2},{5,3},{6,4},{7,5},{8,14},{9,15},{10,... | collective-permute-start | bytes 1277960 | tf_op jit(solution)/shard_map/ppermute | solution.py:238
  71.2 11.8 %collective-permute-start.8 = (bf16[16,2,4,1664]{3,2,1,0:T(4,128)(2,1)S(1)}, bf16[16,2,4,1664]{3,2,1,0:T(4,128)(2,1)S(1)}, u32[]{:S(2)}, u32[]{:S(2)}) collective-permute-start(bf16[16,2,4,1664]{3,2,1,0:T(4,128)(2,1)S(1)} %get-tuple-element.73), channel_id=1, source_target_pairs={{0,2},{1,3},{2,4},{3,5},{4,6},{5,7},{6,0},{7,1},{8,10},{9,11},{10,... | collective-permute-start | bytes 1277960 | tf_op jit(solution)/shard_map/ppermute | solution.py:238
  71.8 11.2 %collective-permute-start.9 = (bf16[16,2,4,1664]{3,2,1,0:T(4,128)(2,1)S(1)}, bf16[16,2,4,1664]{3,2,1,0:T(4,128)(2,1)S(1)}, u32[]{:S(2)}, u32[]{:S(2)}) collective-permute-start(bf16[16,2,4,1664]{3,2,1,0:T(4,128)(2,1)S(1)} %get-tuple-element.74), channel_id=1, source_target_pairs={{0,6},{1,7},{2,0},{3,1},{4,2},{5,3},{6,4},{7,5},{8,14},{9,15},{10,... | collective-permute-start | bytes 1277960 | tf_op jit(solution)/shard_map/ppermute | solution.py:238
  78.4 11.2 %collective-permute-start.6 = (bf16[16,2,4,1664]{3,2,1,0:T(4,128)(2,1)S(1)}, bf16[16,2,4,1664]{3,2,1,0:T(4,128)(2,1)S(1)}, u32[]{:S(2)}, u32[]{:S(2)}) collective-permute-start(bf16[16,2,4,1664]{3,2,1,0:T(4,128)(2,1)S(1)} %get-tuple-element.68), channel_id=1, source_target_pairs={{0,2},{1,3},{2,4},{3,5},{4,6},{5,7},{6,0},{7,1},{8,10},{9,11},{10,... | collective-permute-start | bytes 1277960 | tf_op jit(solution)/shard_map/ppermute | solution.py:238
  78.5 11.3 %collective-permute-start.7 = (bf16[16,2,4,1664]{3,2,1,0:T(4,128)(2,1)S(1)}, bf16[16,2,4,1664]{3,2,1,0:T(4,128)(2,1)S(1)}, u32[]{:S(2)}, u32[]{:S(2)}) collective-permute-start(bf16[16,2,4,1664]{3,2,1,0:T(4,128)(2,1)S(1)} %get-tuple-element.70), channel_id=1, source_target_pairs={{0,6},{1,7},{2,0},{3,1},{4,2},{5,3},{6,4},{7,5},{8,14},{9,15},{10,... | collective-permute-start | bytes 1277960 | tf_op jit(solution)/shard_map/ppermute | solution.py:238
  90.1 10.3 %collective-permute-start.10 = (bf16[16,2,4,1664]{3,2,1,0:T(4,128)(2,1)S(1)}, bf16[16,2,4,1664]{3,2,1,0:T(4,128)(2,1)S(1)}, u32[]{:S(2)}, u32[]{:S(2)}) collective-permute-start(bf16[16,2,4,1664]{3,2,1,0:T(4,128)(2,1)S(1)} %add_convert_fusion.1), channel_id=1, source_target_pairs={{0,2},{1,3},{2,4},{3,5},{4,6},{5,7},{6,0},{7,1},{8,10},{9,11},{10,... | collective-permute-start | bytes 1277960 | tf_op jit(solution)/shard_map/ppermute | solution.py:238
  92.6 8.1 %collective-permute-start.11 = (bf16[16,2,4,1664]{3,2,1,0:T(4,128)(2,1)S(1)}, bf16[16,2,4,1664]{3,2,1,0:T(4,128)(2,1)S(1)}, u32[]{:S(2)}, u32[]{:S(2)}) collective-permute-start(bf16[16,2,4,1664]{3,2,1,0:T(4,128)(2,1)S(1)} %add_convert_fusion), channel_id=1, source_target_pairs={{0,6},{1,7},{2,0},{3,1},{4,2},{5,3},{6,4},{7,5},{8,14},{9,15},{10,... | collective-permute-start | bytes 1277960 | tf_op jit(solution)/shard_map/ppermute | solution.py:238
  93.5 17.0 %collective-permute-start.12 = (bf16[1664,512]{1,0:T(8,128)(2,1)}, bf16[1664,512]{1,0:T(8,128)(2,1)S(1)}, u32[]{:S(2)}, u32[]{:S(2)}) collective-permute-start(bf16[1664,512]{1,0:T(8,128)(2,1)} %get-tuple-element.97), channel_id=1, source_target_pairs={{0,1},{1,0},{2,3},{3,2},{4,5},{5,4},{6,7},{7,6},{8,9},{9,8},{10,11... | collective-permute-start | bytes 5111816 | tf_op jit(solution)/shard_map/ppermute | solution.py:238
  93.5 17.0 %collective-permute-start.13 = (bf16[512,1664]{1,0:T(8,128)(2,1)}, bf16[512,1664]{1,0:T(8,128)(2,1)}, u32[]{:S(2)}, u32[]{:S(2)}) collective-permute-start(bf16[512,1664]{1,0:T(8,128)(2,1)} %get-tuple-element.98), channel_id=1, source_target_pairs={{0,1},{1,0},{2,3},{3,2},{4,5},{5,4},{6,7},{7,6},{8,9},{9,8},{10,11... | collective-permute-start | bytes 5111816 | tf_op jit(solution)/shard_map/ppermute | solution.py:238
  102.1 29.3 %all-to-all-start.1 = ((bf16[32,2,4,1664]{3,2,1,0:T(4,128)(2,1)}), bf16[32,2,4,1664]{3,2,1,0:T(4,128)(2,1)S(1)}, u32[]{:S(2)}, u32[]{:S(2)}) async-start(bf16[32,2,4,1664]{3,2,1,0:T(4,128)(2,1)} %home_sum.1), calls=%async_computation.1 | async-start | bytes 1703936 | tf_op jit(solution)/shard_map/all_to_all | solution.py:241
where the time goes:
time: 136 us
  waiting for transfers between devices  37.9 us (28%)
  blocking collectives  35.6 us (26%)
  Pallas kernels  34.9 us (26%)
  starting transfers between devices  25.9 us (19%)
    all_to_all x1, blocking collectives, exchange(): return lax.all_to_all(rows, 'expert', 0, 0, tiled=True)  35.6 us
    pallas_call x8, Pallas kernels, call(): pl.pallas_call(kernel, out_shape=outs, in_specs=[HBM] * n_s + [VMEM if i...  34.9 us
    ppermute x14, waiting for transfers between devices, send(): return lax.ppermute(array, 'dp', pairs)  24.8 us
    ppermute x14, starting transfers between devices, send(): return lax.ppermute(array, 'dp', pairs)  17.6 us
    all_to_all x1, waiting for transfers between devices, exchange(): return lax.all_to_all(rows, 'expert', 0, 0, tiled=True)  13.1 us
    all_to_all x1, starting transfers between devices, exchange(): return lax.all_to_all(rows, 'expert', 0, 0, tiled=True)  8.36 us
  transfers between devices with their start and end apart: 15, of which 8 were waited for; matrix products, arithmetic and copies ran while one was open for 0% of the time, Pallas kernels for 22%

commit v1 on v0

--- a/solution.py
+++ b/solution.py
@@ -73,7 +73,7 @@
         in_specs=[HBM] * n_s + [VMEM if i in here else HBM for i in range(n_in)],
         out_specs=[VMEM if i in keep else HBM for i in range(n_out)],
         scratch_shapes=buffers + sems + words,
-        compiler_params=pltpu.CompilerParams(vmem_limit_bytes=36 * MIB),
+        compiler_params=pltpu.CompilerParams(vmem_limit_bytes=28 * MIB),
         cost_estimate=pl.CostEstimate(flops=flops, bytes_accessed=moved, transcendentals=0),
         name=name,
     )(*scalars, *ins)
@@ -83,11 +83,10 @@
     return lax.optimization_barrier((values, others))[0]
 
 
-def standardize(floats):
+def moments(floats):
     center = jnp.mean(floats, axis=-1, keepdims=True)
     spread = jnp.mean(jnp.square(floats - center), axis=-1, keepdims=True)
-    inv_std = lax.rsqrt(spread + EPSILON)
-    return (floats - center) * inv_std, inv_std
+    return center, lax.rsqrt(spread + EPSILON)
 
 
 def one_hots(target, slots):
@@ -125,8 +124,11 @@
     block = (experts, CAP, made[0].shape[3])
     rows = gate * jnp.dot(pick, load(4)[...], preferred_element_type=F32)
     made[0][:, 1] = rows.astype(BF16).reshape(block)
-    standard, _ = standardize(load(5)[...].astype(F32))
-    normed = (standard * load(6)[...][None] + load(7)[...][None]).astype(BF16)
+    floats = load(5)[...].astype(F32)
+    center, inv_std = moments(floats)
+    made[2][:, 0:1] = center
+    made[2][:, 1:2] = inv_std
+    normed = ((floats - center) * inv_std * load(6)[...][None] + load(7)[...][None]).astype(BF16)
     rows = jnp.dot(pick, normed, preferred_element_type=F32)
     made[0][:, 0] = rows.astype(BF16).reshape(block)
     store(0)
@@ -202,7 +204,6 @@
 def combine(load, made, store, smem):
     target, gates = load(0)[...], load(1)[...]
     tokens = load(2)[...].astype(F32)
-    standard, inv_std = standardize(tokens)
     home = load(5)
     first, second = one_hots(target, home.shape[0] * CAP)
     rows = rows_of(home, 0)
@@ -216,6 +217,8 @@
     store(0)
     back = lax.dot_general(either(first, second), rows_of(home, 1), TN, preferred_element_type=F32)
     scaled = back * load(3)[...][None]
+    center, inv_std = load(6)[:, 0:1], load(6)[:, 1:2]
+    standard = (tokens - center) * inv_std
     inner = jnp.mean(scaled * standard, axis=-1, keepdims=True)
     centred = scaled - jnp.mean(scaled, axis=-1, keepdims=True) - standard * inner
     made[1][...] = (load(4)[...].astype(F32) + inv_std * centred).astype(BF16)
@@ -247,18 +250,20 @@
     block = sds((experts, 2, CAP, features), BF16)
     half_block = sds((half, 2, CAP, features), BF16)
     small = 2 * slots * n_tok * features
-    in_b, out_b = send(in_a, sibling), send(out_a, sibling)
-    rows, target = call(
+    rows, target, stats = call(
         dispatch,
-        [block, sds((2, n_tok), jnp.int32)],
+        [block, sds((2, n_tok), jnp.int32), sds((n_tok, 2), F32)],
         [expert_t, slot_t, kept_t, gates_t, upstream, tokens, gain, bias],
         scalars=[counts],
-        keep=[0],
+        keep=range(3),
         flops=2 * small,
         name="dispatch",
     )
+    in_b, out_b = after((in_a, out_a), target)
+    in_b, out_b = send(in_b, sibling), send(out_b, sibling)
     rows, in_b, out_b = lax.optimization_barrier((exchange(rows), in_b, out_b))
-    from_right, from_left = send(rows, left), send(rows, right)
+    top, bottom = rows[:half], rows[half:]
+    near = send(top, left), send(bottom, left), send(top, right), send(bottom, right)
 
     def experts_of(blocks, results, name):
         n = sum(b.shape[0] for b in blocks) * CAP
@@ -275,14 +280,12 @@
 
     own_block = sds(block.shape, F32)
     x_own, g_own, own_act_a, own_act_b, own_grad_a, own_grad_b, own = experts_of([rows], [own_block], "own_rows")
-    from_right, from_left, own = lax.optimization_barrier((from_right, from_left, own))
-    far_top, far_bottom = send(from_right[:half], left), send(from_left[half:], right)
+    far_top, far_bottom = send(near[0], left), send(near[3], right)
+    near, own = lax.optimization_barrier((near, own))
     x_near, g_near, act_a, act_b, grad_a, grad_b, right_top, right_bottom, left_top, left_bottom = experts_of(
-        [from_right, from_left], [half_block] * 4, "near_rows"
-    )
-    far_top, far_bottom, right_bottom, left_top = lax.optimization_barrier(
-        (far_top, far_bottom, right_bottom, left_top)
-    )
+        near, [half_block] * 4, "near_rows"
+    )
+    far_top, far_bottom = after((far_top, far_bottom), right_bottom, left_top)
     right_bottom, left_top = send(right_bottom, right), send(left_top, left)
     x_far, g_far, far_act_a, far_act_b, far_grad_a, far_grad_b, far_top, far_bottom = experts_of(
         [far_top, far_bottom], [half_block] * 2, "far_rows"
@@ -321,8 +324,8 @@
     mixed, grad_in = call(
         combine,
         [like, like],
-        [target, gates_t, tokens, gain, upstream, home],
-        here=[5],
+        [target, gates_t, tokens, gain, upstream, home, stats],
+        here=range(7),
         flops=4 * small,
         name="combine",
     )

time: 136 us -> 131 us (0.963)
  waiting for transfers between devices: 37.9 us -> 31.1 us
  local copies, waits for them, and re-layouts: 0.3 us -> 2.95 us
  Pallas kernels: 34.9 us -> 33.3 us
    ppermute x14 -> x16, waiting for transfers between devices: 24.8 us -> 21 us  [send(): return lax.ppermute(array, 'dp', pairs)]
    all_to_all x1, waiting for transfers between devices: 13.1 us -> 10.2 us  [exchange(): return lax.all_to_all(rows, 'expert', 0, 0, tiled=True)]
    unnamed x4 -> x16, local copies, waits for them, and re-layouts: 0.01 us -> 2.66 us
    all_to_all x1, starting transfers between devices: 8.36 us -> 5.95 us  [exchange(): return lax.all_to_all(rows, 'expert', 0, 0, tiled=True)]
    ppermute x14 -> x16, starting transfers between devices: 17.6 us -> 19.6 us  [send(): return lax.ppermute(array, 'dp', pairs)]
    pallas_call x8, Pallas kernels: 34.9 us -> 33.3 us  [call(): pl.pallas_call(kernel, out_shape=outs, in_specs=[HBM] * n_s + [VMEM if i...]
  transfers between devices with their start and end apart: 15 -> 17, of which waited for: 8 -> 8; matrix products, arithmetic and copies ran while one was open for 0% -> 0% of each run, Pallas kernels for 22% -> 21%
where the time goes in v1:
time: 131 us; the launch traced here: 130 us
  blocking collectives  35.7 us (27%)
  Pallas kernels  33.3 us (25%)
  waiting for transfers between devices  31.1 us (24%)
  starting transfers between devices  25.6 us (20%)
  local copies, waits for them, and re-layouts  2.95 us (2%)
    all_to_all x1, blocking collectives, exchange(): return lax.all_to_all(rows, 'expert', 0, 0, tiled=True)  35.7 us
    pallas_call x8, Pallas kernels, call(): pl.pallas_call(kernel, out_shape=outs, in_specs=[HBM] * n_s + [VMEM if i...  33.3 us
    ppermute x16, waiting for transfers between devices, send(): return lax.ppermute(array, 'dp', pairs)  21 us
    ppermute x16, starting transfers between devices, send(): return lax.ppermute(array, 'dp', pairs)  19.6 us
    all_to_all x1, waiting for transfers between devices, exchange(): return lax.all_to_all(rows, 'expert', 0, 0, tiled=True)  10.2 us
    all_to_all x1, starting transfers between devices, exchange(): return lax.all_to_all(rows, 'expert', 0, 0, tiled=True)  5.95 us
    unnamed x16, local copies, waits for them, and re-layouts  2.66 us
  transfers between devices with their start and end apart: 17, of which 8 were waited for; matrix products, arithmetic and copies ran while one was open for 0% of the time, Pallas kernels for 21%

profile of v1, /device:TPU:8, one launch (start us, length us, event | category | flops | bytes accessed | tf_op | source)
XLA Modules:
  0.0 130.2 jit_solution(11408981486439981512)
XLA Ops:
  0.6 2.9 %dispatch.1 = (bf16[32,2,4,1664]{3,2,1,0:T(4,128)(2,1)S(1)}, s32[2,257]{1,0:T(2,128)S(1)}, f32[257,2]{1,0:T(8,128)S(1)}) custom-call(s32[1,32]{1,0:T(1,128)} %refs_0_.1, s32[2,257]{1,0:T(2,128)} %bitcast.18, s32[2,257]{1,0:T(2,128)} %bitcast.19, s32[2,257]{1,0:T(2,128)} %bitcast.20, f32[2,257]{1,0:T(2,128)} %bitcast.16, bf16[257,1664]{1,0:T(8,128)(2,1)} %refs_4_.1, ...), custom_call_target="tpu_custom_call" | custom-call | flops 218955776 | bytes 2588208 | tf_op jit(solution)/shard_map/dispatch/pallas_call | solution.py:70
  3.7 0.5 collective-permute-start.1
  4.2 35.7 %all_to_all.10.refs_0_ = bf16[32,2,4,1664]{3,2,1,0:T(4,128)(2,1)S(1)} all-to-all(bf16[32,2,4,1664]{3,2,1,0:T(4,128)(2,1)S(1)} %get-tuple-element.58), channel_id=1, replica_groups=mesh['expert'=32,'dp'=8] {'expert'}, dimensions={0} | all-to-all | bytes 1703936 | tf_op jit(solution)/shard_map/all_to_all | solution.py:244
  39.9 0.3 fusion
  40.2 1.6 %collective-permute-start.5 = (bf16[16,2,4,1664]{3,2,1,0:T(4,128)(2,1)S(1)}, bf16[16,2,4,1664]{3,2,1,0:T(4,128)(2,1)S(1)}, u32[]{:S(2)}, u32[]{:S(2)}) collective-permute-start(bf16[16,2,4,1664]{3,2,1,0:T(4,128)(2,1)S(1)} %get-tuple-element.110), channel_id=1, source_target_pairs={{0,2},{1,3},{2,4},{3,5},{4,6},{5,7},{6,0},{7,1},{8,10},{9,11},{10,... | collective-permute-start | bytes 1277960 | tf_op jit(solution)/shard_map/ppermute | solution.py:241
  41.8 1.7 %collective-permute-start.2 = (bf16[16,2,4,1664]{3,2,1,0:T(4,128)(2,1)S(1)}, bf16[16,2,4,1664]{3,2,1,0:T(4,128)(2,1)S(1)}, u32[]{:S(2)}, u32[]{:S(2)}) collective-permute-start(bf16[16,2,4,1664]{3,2,1,0:T(4,128)(2,1)S(1)} %get-tuple-element.111), channel_id=1, source_target_pairs={{0,6},{1,7},{2,0},{3,1},{4,2},{5,3},{6,4},{7,5},{8,14},{9,15},{10,... | collective-permute-start | bytes 1277960 | tf_op jit(solution)/shard_map/ppermute | solution.py:241
  43.6 1.5 %collective-permute-start.3 = (bf16[16,2,4,1664]{3,2,1,0:T(4,128)(2,1)S(1)}, bf16[16,2,4,1664]{3,2,1,0:T(4,128)(2,1)S(1)}, u32[]{:S(2)}, u32[]{:S(2)}) collective-permute-start(bf16[16,2,4,1664]{3,2,1,0:T(4,128)(2,1)S(1)} %get-tuple-element.110), channel_id=1, source_target_pairs={{0,6},{1,7},{2,0},{3,1},{4,2},{5,3},{6,4},{7,5},{8,14},{9,15},{10,... | collective-permute-start | bytes 1277960 | tf_op jit(solution)/shard_map/ppermute | solution.py:241
  45.1 0.5 collective-permute-start.4
  45.6 8.7 %collective-permute-done.5.refs_3_ = bf16[16,2,4,1664]{3,2,1,0:T(4,128)(2,1)S(1)} collective-permute-done((bf16[16,2,4,1664]{3,2,1,0:T(4,128)(2,1)S(1)}, bf16[16,2,4,1664]{3,2,1,0:T(4,128)(2,1)S(1)}, u32[]{:S(2)}, u32[]{:S(2)}) %collective-permute-start.5) | collective-permute-done | bytes 426016 | tf_op jit(solution)/shard_map/ppermute | solution.py:241
  54.6 3.0 %collective-permute-start.6 = (bf16[16,2,4,1664]{3,2,1,0:T(4,128)(2,1)S(1)}, bf16[16,2,4,1664]{3,2,1,0:T(4,128)(2,1)S(1)}, u32[]{:S(2)}, u32[]{:S(2)}) collective-permute-start(bf16[16,2,4,1664]{3,2,1,0:T(4,128)(2,1)S(1)} %collective-permute-done.2.refs_0_), channel_id=1, source_target_pairs={{0,6},{1,7},{2,0},{3,1},{4,2},{5,3},{6,4},{7,5},{8,14},{9,15},{10,... | collective-permute-start | bytes 1277960 | tf_op jit(solution)/shard_map/ppermute | solution.py:241
  57.5 3.1 %own_rows.1 = (bf16[128,1664]{1,0:T(8,128)(2,1)}, bf16[128,1664]{1,0:T(8,128)(2,1)}, bf16[128,512]{1,0:T(8,128)(2,1)}, bf16[128,512]{1,0:T(8,128)(2,1)}, bf16[12...) custom-call(bf16[32,2,4,1664]{3,2,1,0:T(4,128)(2,1)S(1)} %all_to_all.10.refs_0_, ...), custom_call_target="tpu_custom_call" | custom-call | flops 1744830464 | bytes 10747904 | tf_op jit(solution)/shard_map/own_rows/pallas_call | solution.py:70
  60.7 3.0 %collective-permute-done.3.refs_1_ = bf16[16,2,4,1664]{3,2,1,0:T(4,128)(2,1)S(1)} collective-permute-done((bf16[16,2,4,1664]{3,2,1,0:T(4,128)(2,1)S(1)}, bf16[16,2,4,1664]{3,2,1,0:T(4,128)(2,1)S(1)}, u32[]{:S(2)}, u32[]{:S(2)}) %collective-permute-start.3) | collective-permute-done | bytes 426016 | tf_op jit(solution)/shard_map/ppermute | solution.py:241
  63.7 4.9 %near_rows.1 = (bf16[256,1664]{1,0:T(8,128)(2,1)}, bf16[256,1664]{1,0:T(8,128)(2,1)}, bf16[256,512]{1,0:T(8,128)(2,1)}, bf16[256,512]{1,0:T(8,128)(2,1)}, bf16[2...) custom-call(bf16[16,2,4,1664]{3,2,1,0:T(4,128)(2,1)S(1)} %collective, ...), custom_call_target="tpu_custom_call" | custom-call | flops 3489660928 | bytes 12976128 | tf_op jit(solution)/shard_map/near_rows/pallas_call | solution.py:70
  68.6 1.6 %collective-permute-start.10 = (bf16[16,2,4,1664]{3,2,1,0:T(4,128)(2,1)S(1)}, bf16[16,2,4,1664]{3,2,1,0:T(4,128)(2,1)S(1)}, u32[]{:S(2)}, u32[]{:S(2)}) collective-permute-start(bf16[16,2,4,1664]{3,2,1,0:T(4,128)(2,1)S(1)} %get-tuple-element.71), channel_id=1, source_target_pairs={{0,2},{1,3},{2,4},{3,5},{4,6},{5,7},{6,0},{7,1},{8,10},{9,11},{10,... | collective-permute-start | bytes 1277960 | tf_op jit(solution)/shard_map/ppermute | solution.py:241
  70.2 1.7 %collective-permute-start.11 = (bf16[16,2,4,1664]{3,2,1,0:T(4,128)(2,1)S(1)}, bf16[16,2,4,1664]{3,2,1,0:T(4,128)(2,1)S(1)}, u32[]{:S(2)}, u32[]{:S(2)}) collective-permute-start(bf16[16,2,4,1664]{3,2,1,0:T(4,128)(2,1)S(1)} %get-tuple-element.72), channel_id=1, source_target_pairs={{0,6},{1,7},{2,0},{3,1},{4,2},{5,3},{6,4},{7,5},{8,14},{9,15},{10,... | collective-permute-start | bytes 1277960 | tf_op jit(solution)/shard_map/ppermute | solution.py:241
  71.9 0.6 collective-permute-done.7.refs_1_
  72.8 4.0 %far_rows.1 = (bf16[128,1664]{1,0:T(8,128)(2,1)}, bf16[128,1664]{1,0:T(8,128)(2,1)}, bf16[128,512]{1,0:T(8,128)(2,1)}, bf16[128,512]{1,0:T(8,128)(2,1)}, bf16[12...) custom-call(bf16[16,2,4,1664]{3,2,1,0:T(4,128)(2,1)S(1)} %collective, ...), custom_call_target="tpu_custom_call" | custom-call | flops 1744830464 | bytes 9895936 | tf_op jit(solution)/shard_map/far_rows/pallas_call | solution.py:70
  76.9 1.6 %collective-permute-start.8 = (bf16[16,2,4,1664]{3,2,1,0:T(4,128)(2,1)S(1)}, bf16[16,2,4,1664]{3,2,1,0:T(4,128)(2,1)S(1)}, u32[]{:S(2)}, u32[]{:S(2)}) collective-permute-start(bf16[16,2,4,1664]{3,2,1,0:T(4,128)(2,1)S(1)} %get-tuple-element.75), channel_id=1, source_target_pairs={{0,2},{1,3},{2,4},{3,5},{4,6},{5,7},{6,0},{7,1},{8,10},{9,11},{10,... | collective-permute-start | bytes 1277960 | tf_op jit(solution)/shard_map/ppermute | solution.py:241
  78.4 1.7 %collective-permute-start.9 = (bf16[16,2,4,1664]{3,2,1,0:T(4,128)(2,1)S(1)}, bf16[16,2,4,1664]{3,2,1,0:T(4,128)(2,1)S(1)}, u32[]{:S(2)}, u32[]{:S(2)}) collective-permute-start(bf16[16,2,4,1664]{3,2,1,0:T(4,128)(2,1)S(1)} %get-tuple-element.77), channel_id=1, source_target_pairs={{0,6},{1,7},{2,0},{3,1},{4,2},{5,3},{6,4},{7,5},{8,14},{9,15},{10,... | collective-permute-start | bytes 1277960 | tf_op jit(solution)/shard_map/ppermute | solution.py:241
  80.2 2.5 %collective-permute-done.10.refs_2_ = bf16[16,2,4,1664]{3,2,1,0:T(4,128)(2,1)S(1)} collective-permute-done((bf16[16,2,4,1664]{3,2,1,0:T(4,128)(2,1)S(1)}, bf16[16,2,4,1664]{3,2,1,0:T(4,128)(2,1)S(1)}, u32[]{:S(2)}, u32[]{:S(2)}) %collective-permute-start.10) | collective-permute-done | bytes 426016 | tf_op jit(solution)/shard_map/ppermute | solution.py:241
  82.9 6.3 %weights_b.1 = (bf16[1664,512]{1,0:T(8,128)(2,1)}, bf16[512,1664]{1,0:T(8,128)(2,1)}) custom-call(bf16[256,1664]{1,0:T(8,128)(2,1)} %get-tuple-element.80.refs_0_, bf16[256,512]{1,0:T(8,128)(2,1)} %get-tuple-element.81.refs_1_, bf16[128,1664]{1,0:T(8,128)(2,1)} %get-tuple-element.82.refs_2_, bf16[128,512]{1,0:T(8,128)(2,1)} %get-tuple-element.83.refs_3_, ...), custom_call_target="tpu_custom_call" | custom-call | flops 1744830464 | bytes 7864320 | tf_op jit(solution)/shard_map/weights_b/pallas_call | solution.py:70
  89.7 1.3 collective-permute-start.12
  91.0 2.0 %collective-permute-start.13 = (bf16[16,2,4,1664]{3,2,1,0:T(4,128)(2,1)S(1)}, bf16[16,2,4,1664]{3,2,1,0:T(4,128)(2,1)S(1)}, u32[]{:S(2)}, u32[]{:S(2)}) collective-permute-start(bf16[16,2,4,1664]{3,2,1,0:T(4,128)(2,1)S(1)} %add_convert_fusion), channel_id=1, source_target_pairs={{0,6},{1,7},{2,0},{3,1},{4,2},{5,3},{6,4},{7,5},{8,14},{9,15},{10,... | collective-permute-start | bytes 1277960 | tf_op jit(solution)/shard_map/ppermute | solution.py:241
  93.0 0.5 collective-permute-start.15
  93.5 5.6 %collective-permute-done.12.refs_1_ = bf16[16,2,4,1664]{3,2,1,0:T(4,128)(2,1)S(1)} collective-permute-done((bf16[16,2,4,1664]{3,2,1,0:T(4,128)(2,1)S(1)}, bf16[16,2,4,1664]{3,2,1,0:T(4,128)(2,1)S(1)}, u32[]{:S(2)}, u32[]{:S(2)}) %collective-permute-start.12) | collective-permute-done | bytes 426016 | tf_op jit(solution)/shard_map/ppermute | solution.py:241
  99.1 1.4 %home_sum.1 = bf16[32,2,4,1664]{3,2,1,0:T(4,128)(2,1)} custom-call(f32[32,2,4,1664]{3,2,1,0:T(4,128)S(1)} %get-tuple-element.65.refs_0_, bf16[16,2,4,1664]{3,2,1,0:T(4,128)(2,1)S(1)} %collective-permute-done.12.refs_1_, bf16[16,2,4,1664]{3,2,1,0:T(4,128)(2,1)S(1)} %collective-permute-done.10.refs_2_, ...), custom_call_target="tpu_custom_call" | custom-call | bytes 4259840 | tf_op jit(solution)/shard_map/home_sum/pallas_call | solution.py:70
  100.5 6.0 %all-to-all-start.1 = ((bf16[32,2,4,1664]{3,2,1,0:T(4,128)(2,1)}), bf16[32,2,4,1664]{3,2,1,0:T(4,128)(2,1)S(1)}, u32[]{:S(2)}, u32[]{:S(2)}) async-start(bf16[32,2,4,1664]{3,2,1,0:T(4,128)(2,1)} %home_sum.1), calls=%async_computation.1 | async-start | bytes 1703936 | tf_op jit(solution)/shard_map/all_to_all | solution.py:244
  106.5 1.2 copy-done.4
  107.7 1.5 %copy-done.5 = bf16[1664,512]{1,0:T(8,128)(2,1)S(1)} copy-done((bf16[1664,512]{1,0:T(8,128)(2,1)S(1)}, bf16[1664,512]{1,0:T(8,128)(2,1)}, u32[]{:S(2)}) %copy-start.5) | copy-done | bytes 1703960
  109.1 7.9 %weights_a.1 = (bf16[1664,512]{1,0:T(8,128)(2,1)}, bf16[512,1664]{1,0:T(8,128)(2,1)}) custom-call(bf16[256,1664]{1,0:T(8,128)(2,1)} %get-tuple-element.80.refs_0_, bf16[256,512]{1,0:T(8,128)(2,1)} %get-tuple-element.96.refs_1_, bf16[128,1664]{1,0:T(8,128)(2,1)} %get-tuple-element.82.refs_2_, bf16[128,512]{1,0:T(8,128)(2,1)} %get-tuple-element.97.refs_3_, ...), custom_call_target="tpu_custom_call" | custom-call | flops 1744830464 | bytes 11272192 | tf_op jit(solution)/shard_map/weights_a/pallas_call | solution.py:70
  117.0 10.2 %all-to-all-done.1.refs_5_ = bf16[32,2,4,1664]{3,2,1,0:T(4,128)(2,1)S(1)} async-done(((bf16[32,2,4,1664]{3,2,1,0:T(4,128)(2,1)}), bf16[32,2,4,1664]{3,2,1,0:T(4,128)(2,1)S(1)}, u32[]{:S(2)}, u32[]{:S(2)}) %all-to-all-start.1) | async-done | bytes 852000 | tf_op jit(solution)/shard_map/all_to_all | solution.py:244
  127.2 2.8 %combine.1 = (bf16[257,1664]{1,0:T(8,128)(2,1)}, bf16[257,1664]{1,0:T(8,128)(2,1)}) custom-call(s32[2,257]{1,0:T(2,128)S(1)} %get-tuple-element.57.refs_0_, f32[2,257]{1,0:T(2,128)S(1)} %bitcast.17, bf16[257,1664]{1,0:T(8,128)(2,1)S(1)} %copy-done.3, f32[1664]{0:T(1024)S(1)} %copy-done.6, bf16[257,1664]{1,0:T(8,128)(2,1)S(1)} %copy-done.2, ...), custom_call_target="tpu_custom_call" | custom-call | flops 437911552 | bytes 4285976 | tf_op jit(solution)/shard_map/combine/pallas_call | solution.py:70
  (30 shorter events, 1.4 us)
Async XLA Ops:
  0.6 3.0 %copy-start = (bf16[1,1664,512]{2,1,0:T(8,128)(2,1)S(1)}, bf16[1,1664,512]{2,1,0:T(8,128)(2,1)}, u32[]{:S(2)}) copy-start(bf16[1,1664,512]{2,1,0:T(8,128)(2,1)} %param.20) | copy-start | bytes 5111812
  3.6 36.3 %collective-permute-start = (bf16[1664,512]{1,0:T(8,128)(2,1)S(1)}, bf16[1664,512]{1,0:T(8,128)(2,1)S(1)}, u32[]{:S(2)}, u32[]{:S(2)}) collective-permute-start(bf16[1664,512]{1,0:T(8,128)(2,1)S(1)} %bitcast.8), channel_id=1, source_target_pairs={{0,1},{1,0},{2,3},{3,2},{4,5},{5,4},{6,7},{7,6},{8,9},{9,8},{10,11... | collective-permute-start | bytes 5111816 | tf_op jit(solution)/shard_map/ppermute | solution.py:241
  3.7 36.2 %collective-permute-start.1 = (bf16[512,1664]{1,0:T(8,128)(2,1)}, bf16[512,1664]{1,0:T(8,128)(2,1)S(1)}, u32[]{:S(2)}, u32[]{:S(2)}) collective-permute-start(bf16[512,1664]{1,0:T(8,128)(2,1)} %bitcast.12), channel_id=1, source_target_pairs={{0,1},{1,0},{2,3},{3,2},{4,5},{5,4},{6,7},{7,6},{8,9},{9,8},{10,11... | collective-permute-start | bytes 5111816 | tf_op jit(solution)/shard_map/ppermute | solution.py:241
  4.2 53.3 %copy-start.1 = (bf16[1,512,1664]{2,1,0:T(8,128)(2,1)S(1)}, bf16[1,512,1664]{2,1,0:T(8,128)(2,1)}, u32[]{:S(2)}) copy-start(bf16[1,512,1664]{2,1,0:T(8,128)(2,1)} %param.21) | copy-start | bytes 5111812
  40.2 14.0 %collective-permute-start.5 = (bf16[16,2,4,1664]{3,2,1,0:T(4,128)(2,1)S(1)}, bf16[16,2,4,1664]{3,2,1,0:T(4,128)(2,1)S(1)}, u32[]{:S(2)}, u32[]{:S(2)}) collective-permute-start(bf16[16,2,4,1664]{3,2,1,0:T(4,128)(2,1)S(1)} %get-tuple-element.110), channel_id=1, source_target_pairs={{0,2},{1,3},{2,4},{3,5},{4,6},{5,7},{6,0},{7,1},{8,10},{9,11},{10,... | collective-permute-start | bytes 1277960 | tf_op jit(solution)/shard_map/ppermute | solution.py:241
  41.8 12.8 %collective-permute-start.2 = (bf16[16,2,4,1664]{3,2,1,0:T(4,128)(2,1)S(1)}, bf16[16,2,4,1664]{3,2,1,0:T(4,128)(2,1)S(1)}, u32[]{:S(2)}, u32[]{:S(2)}) collective-permute-start(bf16[16,2,4,1664]{3,2,1,0:T(4,128)(2,1)S(1)} %get-tuple-element.111), channel_id=1, source_target_pairs={{0,6},{1,7},{2,0},{3,1},{4,2},{5,3},{6,4},{7,5},{8,14},{9,15},{10,... | collective-permute-start | bytes 1277960 | tf_op jit(solution)/shard_map/ppermute | solution.py:241
  43.6 20.1 %collective-permute-start.3 = (bf16[16,2,4,1664]{3,2,1,0:T(4,128)(2,1)S(1)}, bf16[16,2,4,1664]{3,2,1,0:T(4,128)(2,1)S(1)}, u32[]{:S(2)}, u32[]{:S(2)}) collective-permute-start(bf16[16,2,4,1664]{3,2,1,0:T(4,128)(2,1)S(1)} %get-tuple-element.110), channel_id=1, source_target_pairs={{0,6},{1,7},{2,0},{3,1},{4,2},{5,3},{6,4},{7,5},{8,14},{9,15},{10,... | collective-permute-start | bytes 1277960 | tf_op jit(solution)/shard_map/ppermute | solution.py:241
  45.1 18.6 %collective-permute-start.4 = (bf16[16,2,4,1664]{3,2,1,0:T(4,128)(2,1)S(1)}, bf16[16,2,4,1664]{3,2,1,0:T(4,128)(2,1)S(1)}, u32[]{:S(2)}, u32[]{:S(2)}) collective-permute-start(bf16[16,2,4,1664]{3,2,1,0:T(4,128)(2,1)S(1)} %get-tuple-element.111), channel_id=1, source_target_pairs={{0,2},{1,3},{2,4},{3,5},{4,6},{5,7},{6,0},{7,1},{8,10},{9,11},{10,... | collective-permute-start | bytes 1277960 | tf_op jit(solution)/shard_map/ppermute | solution.py:241
  54.3 18.3 %collective-permute-start.7 = (bf16[16,2,4,1664]{3,2,1,0:T(4,128)(2,1)S(1)}, bf16[16,2,4,1664]{3,2,1,0:T(4,128)(2,1)S(1)}, u32[]{:S(2)}, u32[]{:S(2)}) collective-permute-start(bf16[16,2,4,1664]{3,2,1,0:T(4,128)(2,1)S(1)} %collective-permute-done.5.refs_3_), channel_id=1, source_target_pairs={{0,2},{1,3},{2,4},{3,5},{4,6},{5,7},{6,0},{7,1},{8,10},{9,11},{10,... | collective-permute-start | bytes 1277960 | tf_op jit(solution)/shard_map/ppermute | solution.py:241
  54.6 18.3 %collective-permute-start.6 = (bf16[16,2,4,1664]{3,2,1,0:T(4,128)(2,1)S(1)}, bf16[16,2,4,1664]{3,2,1,0:T(4,128)(2,1)S(1)}, u32[]{:S(2)}, u32[]{:S(2)}) collective-permute-start(bf16[16,2,4,1664]{3,2,1,0:T(4,128)(2,1)S(1)} %collective-permute-done.2.refs_0_), channel_id=1, source_target_pairs={{0,6},{1,7},{2,0},{3,1},{4,2},{5,3},{6,4},{7,5},{8,14},{9,15},{10,... | collective-permute-start | bytes 1277960 | tf_op jit(solution)/shard_map/ppermute | solution.py:241
  68.6 14.0 %collective-permute-start.10 = (bf16[16,2,4,1664]{3,2,1,0:T(4,128)(2,1)S(1)}, bf16[16,2,4,1664]{3,2,1,0:T(4,128)(2,1)S(1)}, u32[]{:S(2)}, u32[]{:S(2)}) collective-permute-start(bf16[16,2,4,1664]{3,2,1,0:T(4,128)(2,1)S(1)} %get-tuple-element.71), channel_id=1, source_target_pairs={{0,2},{1,3},{2,4},{3,5},{4,6},{5,7},{6,0},{7,1},{8,10},{9,11},{10,... | collective-permute-start | bytes 1277960 | tf_op jit(solution)/shard_map/ppermute | solution.py:241
  70.2 12.8 %collective-permute-start.11 = (bf16[16,2,4,1664]{3,2,1,0:T(4,128)(2,1)S(1)}, bf16[16,2,4,1664]{3,2,1,0:T(4,128)(2,1)S(1)}, u32[]{:S(2)}, u32[]{:S(2)}) collective-permute-start(bf16[16,2,4,1664]{3,2,1,0:T(4,128)(2,1)S(1)} %get-tuple-element.72), channel_id=1, source_target_pairs={{0,6},{1,7},{2,0},{3,1},{4,2},{5,3},{6,4},{7,5},{8,14},{9,15},{10,... | collective-permute-start | bytes 1277960 | tf_op jit(solution)/shard_map/ppermute | solution.py:241
  76.9 12.4 %collective-permute-start.8 = (bf16[16,2,4,1664]{3,2,1,0:T(4,128)(2,1)S(1)}, bf16[16,2,4,1664]{3,2,1,0:T(4,128)(2,1)S(1)}, u32[]{:S(2)}, u32[]{:S(2)}) collective-permute-start(bf16[16,2,4,1664]{3,2,1,0:T(4,128)(2,1)S(1)} %get-tuple-element.75), channel_id=1, source_target_pairs={{0,2},{1,3},{2,4},{3,5},{4,6},{5,7},{6,0},{7,1},{8,10},{9,11},{10,... | collective-permute-start | bytes 1277960 | tf_op jit(solution)/shard_map/ppermute | solution.py:241
  78.4 11.0 %collective-permute-start.9 = (bf16[16,2,4,1664]{3,2,1,0:T(4,128)(2,1)S(1)}, bf16[16,2,4,1664]{3,2,1,0:T(4,128)(2,1)S(1)}, u32[]{:S(2)}, u32[]{:S(2)}) collective-permute-start(bf16[16,2,4,1664]{3,2,1,0:T(4,128)(2,1)S(1)} %get-tuple-element.77), channel_id=1, source_target_pairs={{0,6},{1,7},{2,0},{3,1},{4,2},{5,3},{6,4},{7,5},{8,14},{9,15},{10,... | collective-permute-start | bytes 1277960 | tf_op jit(solution)/shard_map/ppermute | solution.py:241
  89.7 9.4 %collective-permute-start.12 = (bf16[16,2,4,1664]{3,2,1,0:T(4,128)(2,1)S(1)}, bf16[16,2,4,1664]{3,2,1,0:T(4,128)(2,1)S(1)}, u32[]{:S(2)}, u32[]{:S(2)}) collective-permute-start(bf16[16,2,4,1664]{3,2,1,0:T(4,128)(2,1)S(1)} %add_convert_fusion.1), channel_id=1, source_target_pairs={{0,2},{1,3},{2,4},{3,5},{4,6},{5,7},{6,0},{7,1},{8,10},{9,11},{10,... | collective-permute-start | bytes 1277960 | tf_op jit(solution)/shard_map/ppermute | solution.py:241
  91.0 8.1 %collective-permute-start.13 = (bf16[16,2,4,1664]{3,2,1,0:T(4,128)(2,1)S(1)}, bf16[16,2,4,1664]{3,2,1,0:T(4,128)(2,1)S(1)}, u32[]{:S(2)}, u32[]{:S(2)}) collective-permute-start(bf16[16,2,4,1664]{3,2,1,0:T(4,128)(2,1)S(1)} %add_convert_fusion), channel_id=1, source_target_pairs={{0,6},{1,7},{2,0},{3,1},{4,2},{5,3},{6,4},{7,5},{8,14},{9,15},{10,... | collective-permute-start | bytes 1277960 | tf_op jit(solution)/shard_map/ppermute | solution.py:241
  93.0 13.4 %collective-permute-start.14 = (bf16[1664,512]{1,0:T(8,128)(2,1)}, bf16[1664,512]{1,0:T(8,128)(2,1)S(1)}, u32[]{:S(2)}, u32[]{:S(2)}) collective-permute-start(bf16[1664,512]{1,0:T(8,128)(2,1)} %get-tuple-element.102), channel_id=1, source_target_pairs={{0,1},{1,0},{2,3},{3,2},{4,5},{5,4},{6,7},{7,6},{8,9},{9,8},{10,11... | collective-permute-start | bytes 5111816 | tf_op jit(solution)/shard_map/ppermute | solution.py:241
  93.0 14.6 %collective-permute-start.15 = (bf16[512,1664]{1,0:T(8,128)(2,1)}, bf16[512,1664]{1,0:T(8,128)(2,1)}, u32[]{:S(2)}, u32[]{:S(2)}) collective-permute-start(bf16[512,1664]{1,0:T(8,128)(2,1)} %get-tuple-element.103), channel_id=1, source_target_pairs={{0,1},{1,0},{2,3},{3,2},{4,5},{5,4},{6,7},{7,6},{8,9},{9,8},{10,11... | collective-permute-start | bytes 5111816 | tf_op jit(solution)/shard_map/ppermute | solution.py:241
  100.5 26.7 %all-to-all-start.1 = ((bf16[32,2,4,1664]{3,2,1,0:T(4,128)(2,1)}), bf16[32,2,4,1664]{3,2,1,0:T(4,128)(2,1)S(1)}, u32[]{:S(2)}, u32[]{:S(2)}) async-start(bf16[32,2,4,1664]{3,2,1,0:T(4,128)(2,1)} %home_sum.1), calls=%async_computation.1 | async-start | bytes 1703936 | tf_op jit(solution)/shard_map/all_to_all | solution.py:244
  106.5 1.2 copy-start.4
  107.7 1.5 %copy-start.5 = (bf16[1664,512]{1,0:T(8,128)(2,1)S(1)}, bf16[1664,512]{1,0:T(8,128)(2,1)}, u32[]{:S(2)}) copy-start(bf16[1664,512]{1,0:T(8,128)(2,1)} %copy-done.4) | copy-start | bytes 5111812
  109.1 18.1 %copy-start.2 = (bf16[257,1664]{1,0:T(8,128)(2,1)S(1)}, bf16[257,1664]{1,0:T(8,128)(2,1)}, u32[]{:S(2)}) copy-start(bf16[257,1664]{1,0:T(8,128)(2,1)} %refs_4_.1) | copy-start | bytes 2565892
  109.1 18.1 %copy-start.3 = (bf16[257,1664]{1,0:T(8,128)(2,1)S(1)}, bf16[257,1664]{1,0:T(8,128)(2,1)}, u32[]{:S(2)}) copy-start(bf16[257,1664]{1,0:T(8,128)(2,1)} %refs_2_.1) | copy-start | bytes 2565892
  109.1 18.1 %copy-start.6 = (f32[1664]{0:T(1024)S(1)}, f32[1664]{0:T(1024)}, u32[]{:S(2)}) copy-start(f32[1664]{0:T(1024)} %refs_3_.1) | copy-start | bytes 19972
  109.1 18.1 %copy-start.7 = (f32[257,2]{0,1:T(2,128)S(1)}, f32[257,2]{0,1:T(2,128)}, u32[]{:S(2)}) copy-start(f32[257,2]{0,1:T(2,128)} %param.13) | copy-start | bytes 6172

commit v2 on v1

--- a/solution.py
+++ b/solution.py
@@ -21,21 +21,29 @@
 
 def call(body, outs, ins, scalars=(), here=(), keep=(), flops=0, name=None):
     n_in, n_out, n_s = len(ins), len(outs), len(scalars)
+    ins = [list(a) if isinstance(a, (list, tuple)) else [a] for a in ins]
+    flat_in = [a for group in ins for a in group]
+    first = [sum(len(g) for g in ins[:i]) for i in range(n_in)]
     far_in = [i for i in range(n_in) if i not in here]
     far_out = [i for i in range(n_out) if i not in keep]
 
     def kernel(*refs):
         words, refs = refs[:n_s], refs[n_s:]
-        source, refs = refs[:n_in], refs[n_in:]
+        source, refs = refs[: len(flat_in)], refs[len(flat_in) :]
         sink, refs = refs[:n_out], refs[n_out:]
         held, refs = dict(zip(far_in, refs)), refs[len(far_in) :]
         made, refs = dict(zip(far_out, refs)), refs[len(far_out) :]
         in_sem, out_sem, word_sem, *smem = refs
         word_copies = [pltpu.make_async_copy(a, b, word_sem.at[k]) for k, (a, b) in enumerate(zip(words, smem))]
-        for c in word_copies:
-            c.start()
-        copies = {i: pltpu.make_async_copy(source[i], held[i], in_sem.at[k]) for k, i in enumerate(far_in)}
-        for c in copies.values():
+        copies = {}
+        for i in far_in:
+            at, copies[i] = 0, []
+            for k in range(first[i], first[i] + len(ins[i])):
+                n = flat_in[k].shape[0]
+                target = held[i] if len(ins[i]) == 1 else held[i].at[pl.ds(at, n)]
+                copies[i].append(pltpu.make_async_copy(source[k], target, in_sem.at[k]))
+                at += n
+        for c in word_copies + [c for group in copies.values() for c in group]:
             c.start()
         for c in word_copies:
             c.wait()
@@ -43,10 +51,11 @@
 
         def load(i):
             if i not in copies:
-                return source[i]
+                return source[first[i]]
             if i not in waited:
                 waited.add(i)
-                copies[i].wait()
+                for c in copies[i]:
+                    c.wait()
             return held[i]
 
         def store(i):
@@ -59,24 +68,28 @@
         for c in sent:
             c.wait()
 
-    moved = sum(a.size * a.dtype.itemsize for a in list(outs) + list(ins))
-    buffers = [pltpu.VMEM(ins[i].shape, ins[i].dtype) for i in far_in]
+    moved = sum(a.size * a.dtype.itemsize for a in list(outs) + flat_in)
+    buffers = [pltpu.VMEM((sum(a.shape[0] for a in ins[i]),) + ins[i][0].shape[1:], ins[i][0].dtype) for i in far_in]
     buffers += [pltpu.VMEM(outs[i].shape, outs[i].dtype) for i in far_out]
-    sems = [pltpu.SemaphoreType.DMA((max(1, len(k)),)) for k in (far_in, far_out, scalars)]
-    words = [pltpu.SMEM(a.shape, a.dtype) for a in scalars]
+    sems = [pltpu.SemaphoreType.DMA((max(1, k),)) for k in (len(flat_in), len(far_out), n_s)]
+    smem_words = [pltpu.SMEM(a.shape, a.dtype) for a in scalars]
     scalars = [pltpu.with_memory_space_constraint(a, pltpu.HBM) for a in scalars]
-    ins = [a if i in here else pltpu.with_memory_space_constraint(a, pltpu.HBM) for i, a in enumerate(ins)]
+    given, specs = [], [HBM] * n_s
+    for i, group in enumerate(ins):
+        for a in group:
+            given.append(a if i in here else pltpu.with_memory_space_constraint(a, pltpu.HBM))
+            specs.append(VMEM if i in here else HBM)
     outs = [o if i in keep else pltpu.HBM(o.shape, o.dtype) for i, o in enumerate(outs)]
     return pl.pallas_call(
         kernel,
         out_shape=outs,
-        in_specs=[HBM] * n_s + [VMEM if i in here else HBM for i in range(n_in)],
+        in_specs=specs,
         out_specs=[VMEM if i in keep else HBM for i in range(n_out)],
-        scratch_shapes=buffers + sems + words,
+        scratch_shapes=buffers + sems + smem_words,
         compiler_params=pltpu.CompilerParams(vmem_limit_bytes=28 * MIB),
         cost_estimate=pl.CostEstimate(flops=flops, bytes_accessed=moved, transcendentals=0),
         name=name,
-    )(*scalars, *ins)
+    )(*scalars, *given)
 
 
 def after(values, *others):
@@ -89,9 +102,23 @@
     return center, lax.rsqrt(spread + EPSILON)
 
 
-def one_hots(target, slots):
-    rows = lax.broadcasted_iota(jnp.int32, (slots, target.shape[1]), 0)
-    return rows == target[0:1], rows == target[1:2]
+def one_hots(target, rows, part):
+    row = lax.broadcasted_iota(jnp.int32, (rows, target.shape[1]), 0)
+    slot = jnp.where(row // CAP % 2 == part, row // (2 * CAP) * CAP + row % CAP, -1)
+    return slot == target[0:1], slot == target[1:2]
+
+
+def travelling(index, rows):
+    part = jnp.where(index < rows // 2, 0, 1)
+    i = index - part * (rows // 2)
+    return i // CAP * (2 * CAP) + part * CAP + i % CAP
+
+
+def permutation(rows, apart):
+    down = lax.broadcasted_iota(jnp.int32, (rows, rows), 0)
+    across = lax.broadcasted_iota(jnp.int32, (rows, rows), 1)
+    here = travelling(down, rows) == across if apart else travelling(across, rows) == down
+    return jnp.where(here, 1.0, 0.0).astype(BF16)
 
 
 def either(first, second):
@@ -100,10 +127,6 @@
 
 def weighted(first, second, gates):
     return jnp.where(first, gates[0:1], 0.0) + jnp.where(second, gates[1:2], 0.0)
-
-
-def rows_of(ref, part):
-    return ref[:, part].reshape(ref.shape[0] * ref.shape[2], ref.shape[3])
 
 
 def dispatch(load, made, store, smem):
@@ -118,31 +141,32 @@
     target = jnp.where(active, chosen * CAP + slot, slots)
     made[1][...] = target
     store(1)
-    first, second = one_hots(target, slots)
-    pick = either(first, second)
+    rows = made[0].shape[0]
+    first, second = one_hots(target, rows, 1)
     gate = jnp.sum(weighted(first, second, load(3)[...]), axis=1, keepdims=True)
-    block = (experts, CAP, made[0].shape[3])
-    rows = gate * jnp.dot(pick, load(4)[...], preferred_element_type=F32)
-    made[0][:, 1] = rows.astype(BF16).reshape(block)
+    total = gate * jnp.dot(either(first, second), load(4)[...], preferred_element_type=F32)
     floats = load(5)[...].astype(F32)
     center, inv_std = moments(floats)
     made[2][:, 0:1] = center
     made[2][:, 1:2] = inv_std
     normed = ((floats - center) * inv_std * load(6)[...][None] + load(7)[...][None]).astype(BF16)
-    rows = jnp.dot(pick, normed, preferred_element_type=F32)
-    made[0][:, 0] = rows.astype(BF16).reshape(block)
-    store(0)
+    pick = either(*one_hots(target, rows, 0))
+    total = total + jnp.dot(pick, normed, preferred_element_type=F32)
+    made[0][...] = total.astype(BF16)
 
 
 def expert_rows(n, load, made, store, smem):
     x_all, g_all = made[0], made[1]
-    for part, out in ((0, x_all), (1, g_all)):
-        at = 0
-        for i in range(n):
-            rows = rows_of(load(i), part)
-            out[pl.ds(at, rows.shape[0]), :] = rows
-            at += rows.shape[0]
-        store(part)
+    at = 0
+    for i in range(n):
+        block = load(i)[...]
+        rows = block.shape[0]
+        kinds = jnp.dot(permutation(rows, True), block, preferred_element_type=F32).astype(BF16)
+        x_all[pl.ds(at, rows // 2), :] = kinds[: rows // 2]
+        g_all[pl.ds(at, rows // 2), :] = kinds[rows // 2 :]
+        at += rows // 2
+    store(0)
+    store(1)
     c = 0.7978845608028654
     out, back = None, None
     for k in range(2):
@@ -161,34 +185,26 @@
         out = term if out is None else out + term
         term = lax.dot_general(grad[...], w_in[...], NT, preferred_element_type=F32)
         back = term if back is None else back + term
+    out, back = out.astype(BF16), back.astype(BF16)
     at = 0
     for i in range(6, len(made)):
-        ref = made[i]
-        size = ref.shape[0] * CAP
-        for part, total in ((0, out), (1, back)):
-            piece = total[at : at + size].astype(ref.dtype)
-            ref[:, part] = piece.reshape(ref.shape[0], CAP, ref.shape[3])
-        store(i)
-        at += size
-
-
-def tall_product(load, first):
-    total = None
-    for i in (first, first + 2, first + 4):
-        term = lax.dot_general(load(i)[...], load(i + 1)[...], TN, preferred_element_type=F32)
-        total = term if total is None else total + term
-    return total
+        rows = made[i].shape[0]
+        kinds = jnp.concatenate([out[at : at + rows // 2], back[at : at + rows // 2]], 0)
+        made[i][...] = jnp.dot(permutation(rows, False), kinds, preferred_element_type=F32).astype(BF16)
+        at += rows // 2
 
 
 def weight_grads(load, made, store, smem):
     for k in range(2):
-        made[k][...] = tall_product(load, 6 * k).astype(BF16)
+        total = lax.dot_general(load(2 * k)[...], load(2 * k + 1)[...], TN, preferred_element_type=F32)
+        made[k][...] = total.astype(BF16)
         store(k)
 
 
 def weight_sums(load, made, store, smem):
     for k in range(2):
-        made[k][...] = (tall_product(load, 6 * k) + load(12 + k)[...].astype(F32)).astype(BF16)
+        total = lax.dot_general(load(2 * k)[...], load(2 * k + 1)[...], TN, preferred_element_type=F32)
+        made[k][...] = (total + load(4 + k)[...].astype(F32)).astype(BF16)
         store(k)
 
 
@@ -196,8 +212,8 @@
     half = made[0].shape[0] // 2
     for k in range(2):
         part = pl.ds(k * half, half)
-        total = load(0)[part] + load(1 + k)[...].astype(F32) + load(3 + k)[...].astype(F32)
-        made[0][part] = total.astype(BF16)
+        total = load(0)[part, :].astype(F32) + load(1 + k)[...].astype(F32) + load(3 + k)[...].astype(F32)
+        made[0][part, :] = total.astype(BF16)
     store(0)
 
 
@@ -205,9 +221,8 @@
     target, gates = load(0)[...], load(1)[...]
     tokens = load(2)[...].astype(F32)
     home = load(5)
-    first, second = one_hots(target, home.shape[0] * CAP)
-    rows = rows_of(home, 0)
-    weight = weighted(first, second, gates)
+    rows = home[...]
+    weight = weighted(*one_hots(target, rows.shape[0], 0), gates)
     total = tokens
     for _ in range(3):
         part = weight.astype(BF16)
@@ -215,7 +230,8 @@
         total = total + lax.dot_general(part, rows, TN, preferred_element_type=F32)
     made[0][...] = total.astype(BF16)
     store(0)
-    back = lax.dot_general(either(first, second), rows_of(home, 1), TN, preferred_element_type=F32)
+    pick = either(*one_hots(target, rows.shape[0], 1))
+    back = lax.dot_general(pick, rows, TN, preferred_element_type=F32)
     scaled = back * load(3)[...][None]
     center, inv_std = load(6)[:, 0:1], load(6)[:, 1:2]
     standard = (tokens - center) * inv_std
@@ -231,7 +247,7 @@
     n_tok, features = tokens.shape
     in_a, out_a = in_weight[0], out_weight[0]
     hidden = in_a.shape[1]
-    half = experts // 2
+    half = slots
     n_rows = slots * n_dp // 2
     right = [(i, (i + 2) % n_dp) for i in range(n_dp)]
     left = [(i, (i - 2) % n_dp) for i in range(n_dp)]
@@ -241,14 +257,15 @@
         return lax.ppermute(array, "dp", pairs)
 
     def exchange(rows):
-        return lax.all_to_all(rows, "expert", 0, 0, tiled=True)
+        rows = rows.reshape(experts, 2 * CAP, features)
+        return lax.all_to_all(rows, "expert", 0, 0, tiled=True).reshape(2 * slots, features)
 
     def add(a, b):
         return (a.astype(F32) + b.astype(F32)).astype(BF16)
 
     gates_t, expert_t, slot_t, kept_t = gates.T, expert.T, slot.T, kept.T
-    block = sds((experts, 2, CAP, features), BF16)
-    half_block = sds((half, 2, CAP, features), BF16)
+    block = sds((2 * slots, features), BF16)
+    half_block = sds((half, features), BF16)
     small = 2 * slots * n_tok * features
     rows, target, stats = call(
         dispatch,
@@ -259,14 +276,13 @@
         flops=2 * small,
         name="dispatch",
     )
-    in_b, out_b = after((in_a, out_a), target)
-    in_b, out_b = send(in_b, sibling), send(out_b, sibling)
+    in_b, out_b = send(in_a, sibling), send(out_a, sibling)
     rows, in_b, out_b = lax.optimization_barrier((exchange(rows), in_b, out_b))
     top, bottom = rows[:half], rows[half:]
     near = send(top, left), send(bottom, left), send(top, right), send(bottom, right)
 
     def experts_of(blocks, results, name):
-        n = sum(b.shape[0] for b in blocks) * CAP
+        n = sum(b.shape[0] for b in blocks) // 2
         wide, narrow = sds((n, features), BF16), sds((n, hidden), BF16)
         return call(
             functools.partial(expert_rows, len(blocks)),
@@ -278,8 +294,7 @@
             name=name,
         )
 
-    own_block = sds(block.shape, F32)
-    x_own, g_own, own_act_a, own_act_b, own_grad_a, own_grad_b, own = experts_of([rows], [own_block], "own_rows")
+    x_own, g_own, own_act_a, own_act_b, own_grad_a, own_grad_b, own = experts_of([rows], [block], "own_rows")
     far_top, far_bottom = send(near[0], left), send(near[3], right)
     near, own = lax.optimization_barrier((near, own))
     x_near, g_near, act_a, act_b, grad_a, grad_b, right_top, right_bottom, left_top, left_bottom = experts_of(
@@ -293,14 +308,12 @@
     far_top, far_bottom = send(far_top, right), send(far_bottom, left)
     first, second = sds(in_a.shape, BF16), sds(out_a.shape, BF16)
     flops = 4 * n_rows * features * hidden
+    x_near, grad_b = after((x_near, grad_b), right_bottom, left_top)
+    x_all, g_all = [x_near, x_far, x_own], [g_near, g_far, g_own]
+    act_b, grad_b = [act_b, far_act_b, own_act_b], [grad_b, far_grad_b, own_grad_b]
+    act_a, grad_a = [act_a, far_act_a, own_act_a], [grad_a, far_grad_a, own_grad_a]
     first_b, second_b = call(
-        weight_grads,
-        [first, second],
-        after([x_near, grad_b], right_bottom, left_top)
-        + [x_far, far_grad_b, x_own, own_grad_b, act_b, g_near, far_act_b, g_far, own_act_b, g_own],
-        keep=range(2),
-        flops=flops,
-        name="weights_b",
+        weight_grads, [first, second], [x_all, grad_b, act_b, g_all], keep=range(2), flops=flops, name="weights_b"
     )
     right_top, left_bottom, first_b, second_b = lax.optimization_barrier(
         (add(right_top, far_top), add(left_bottom, far_bottom), first_b, second_b)
@@ -313,9 +326,8 @@
     grad_first, grad_second = call(
         weight_sums,
         [first, second],
-        [x_near, grad_a, x_far, far_grad_a, x_own, own_grad_a]
-        + [act_a, g_near, far_act_a, g_far, own_act_a, g_own, more_first, more_second],
-        here=(12, 13),
+        [x_all, grad_a, act_a, g_all, more_first, more_second],
+        here=(4, 5),
         flops=flops,
         name="weights_a",
     )

time: 131 us -> 131 us (level)
    ppermute x16, waiting for transfers between devices: 21 us -> 19.4 us  [send(): return lax.ppermute(array, 'dp', pairs)]
  transfers between devices with their start and end apart: 17 -> 17, of which waited for: 8 -> 6; matrix products, arithmetic and copies ran while one was open for 0% -> 0% of each run, Pallas kernels for 21% -> 24%
where the time goes in v2:
time: 131 us
  blocking collectives  35.9 us (27%)
  Pallas kernels  34.4 us (26%)
  waiting for transfers between devices  30.7 us (23%)
  starting transfers between devices  25.7 us (20%)
  local copies, waits for them, and re-layouts  2.72 us (2%)
    all_to_all x1, blocking collectives, exchange(): lax.all_to_all(rows, 'expert', 0, 0, tiled=True)  35.9 us
    pallas_call x8, Pallas kernels, call(): pl.pallas_call(kernel, out_shape=outs, in_specs=specs, out_specs=[VMEM if...  34.4 us
    ppermute x16, starting transfers between devices, send(): return lax.ppermute(array, 'dp', pairs)  19.8 us
    ppermute x16, waiting for transfers between devices, send(): return lax.ppermute(array, 'dp', pairs)  19.4 us
    all_to_all x1, waiting for transfers between devices, exchange(): lax.all_to_all(rows, 'expert', 0, 0, tiled=True)  11.3 us
    all_to_all x1, starting transfers between devices, exchange(): lax.all_to_all(rows, 'expert', 0, 0, tiled=True)  5.89 us
    unnamed x16, local copies, waits for them, and re-layouts  2.66 us
  transfers between devices with their start and end apart: 17, of which 6 were waited for; matrix products, arithmetic and copies ran while one was open for 0% of the time, Pallas kernels for 24%

profile of v2, /device:TPU:8, one launch (start us, length us, event | category | flops | bytes accessed | tf_op | source)
XLA Modules:
  0.0 130.6 jit_solution(251774966065760289)
XLA Ops:
  0.7 0.5 collective-permute-start.1
  1.2 3.3 %dispatch.1 = (bf16[256,1664]{1,0:T(8,128)(2,1)S(1)}, s32[2,257]{1,0:T(2,128)S(1)}, f32[257,2]{1,0:T(8,128)S(1)}) custom-call(s32[1,32]{1,0:T(1,128)} %refs_0_.1, s32[2,257]{1,0:T(2,128)} %bitcast.26, s32[2,257]{1,0:T(2,128)} %bitcast.27, s32[2,257]{1,0:T(2,128)} %bitcast.28, f32[2,257]{1,0:T(2,128)} %bitcast.24, bf16[257,1664]{1,0:T(8,128)(2,1)} %refs_4_.1, ...), custom_call_target="tpu_custom_call" | custom-call | flops 218955776 | bytes 2588208 | tf_op jit(solution)/shard_map/dispatch/pallas_call | solution.py:83
  4.6 35.9 %all_to_all.10 = bf16[32,8,1664]{2,1,0:T(8,128)(2,1)S(1)} all-to-all(bf16[32,8,1664]{2,1,0:T(8,128)(2,1)S(1)} %bitcast.23), channel_id=1, replica_groups=mesh['expert'=32,'dp'=8] {'expert'}, dimensions={0} | all-to-all | bytes 1703936 | tf_op jit(solution)/shard_map/all_to_all | solution.py:261
  40.5 1.6 %collective-permute-start.5 = (bf16[128,1664]{1,0:T(8,128)(2,1)S(1)}, bf16[128,1664]{1,0:T(8,128)(2,1)S(1)}, u32[]{:S(2)}, u32[]{:S(2)}) collective-permute-start(bf16[128,1664]{1,0:T(8,128)(2,1)S(1)} %get-tuple-element.106), channel_id=1, source_target_pairs={{0,2},{1,3},{2,4},{3,5},{4,6},{5,7},{6,0},{7,1},{8,10},{9,11},{10,... | collective-permute-start | bytes 1277960 | tf_op jit(solution)/shard_map/ppermute | solution.py:257
  42.1 1.7 %collective-permute-start.2 = (bf16[128,1664]{1,0:T(8,128)(2,1)S(1)}, bf16[128,1664]{1,0:T(8,128)(2,1)S(1)}, u32[]{:S(2)}, u32[]{:S(2)}) collective-permute-start(bf16[128,1664]{1,0:T(8,128)(2,1)S(1)} %get-tuple-element.107), channel_id=1, source_target_pairs={{0,6},{1,7},{2,0},{3,1},{4,2},{5,3},{6,4},{7,5},{8,14},{9,15},{10,... | collective-permute-start | bytes 1277960 | tf_op jit(solution)/shard_map/ppermute | solution.py:257
  43.8 1.5 %collective-permute-start.3 = (bf16[128,1664]{1,0:T(8,128)(2,1)S(1)}, bf16[128,1664]{1,0:T(8,128)(2,1)S(1)}, u32[]{:S(2)}, u32[]{:S(2)}) collective-permute-start(bf16[128,1664]{1,0:T(8,128)(2,1)S(1)} %get-tuple-element.106), channel_id=1, source_target_pairs={{0,6},{1,7},{2,0},{3,1},{4,2},{5,3},{6,4},{7,5},{8,14},{9,15},{10,... | collective-permute-start | bytes 1277960 | tf_op jit(solution)/shard_map/ppermute | solution.py:257
  45.4 0.5 collective-permute-start.4
  45.9 8.7 %collective-permute-done.5.refs_3_ = bf16[128,1664]{1,0:T(8,128)(2,1)S(1)} collective-permute-done((bf16[128,1664]{1,0:T(8,128)(2,1)S(1)}, bf16[128,1664]{1,0:T(8,128)(2,1)S(1)}, u32[]{:S(2)}, u32[]{:S(2)}) %collective-permute-start.5) | collective-permute-done | bytes 426016 | tf_op jit(solution)/shard_map/ppermute | solution.py:257
  54.6 0.3 collective-permute-start.7
  54.8 3.0 %collective-permute-start.6 = (bf16[128,1664]{1,0:T(8,128)(2,1)S(1)}, bf16[128,1664]{1,0:T(8,128)(2,1)S(1)}, u32[]{:S(2)}, u32[]{:S(2)}) collective-permute-start(bf16[128,1664]{1,0:T(8,128)(2,1)S(1)} %collective-permute-done.2.refs_0_), channel_id=1, source_target_pairs={{0,6},{1,7},{2,0},{3,1},{4,2},{5,3},{6,4},{7,5},{8,14},{9,15},{10,... | collective-permute-start | bytes 1277960 | tf_op jit(solution)/shard_map/ppermute | solution.py:257
  57.8 4.4 %own_rows.1 = (bf16[128,1664]{1,0:T(8,128)(2,1)}, bf16[128,1664]{1,0:T(8,128)(2,1)}, bf16[128,512]{1,0:T(8,128)(2,1)}, bf16[128,512]{1,0:T(8,128)(2,1)}, bf16[12...) custom-call(bf16[256,1664]{1,0:T(8,128)(2,1)S(1)} %bitcast.13, ...), custom_call_target="tpu_custom_call" | custom-call | flops 1744830464 | bytes 9895936 | tf_op jit(solution)/shard_map/own_rows/pallas_call | solution.py:83
  62.2 1.8 %collective-permute-done.3.refs_1_ = bf16[128,1664]{1,0:T(8,128)(2,1)S(1)} collective-permute-done((bf16[128,1664]{1,0:T(8,128)(2,1)S(1)}, bf16[128,1664]{1,0:T(8,128)(2,1)S(1)}, u32[]{:S(2)}, u32[]{:S(2)}) %collective-permute-start.3) | collective-permute-done | bytes 426016 | tf_op jit(solution)/shard_map/ppermute | solution.py:257
  64.0 6.2 %near_rows.1 = (bf16[256,1664]{1,0:T(8,128)(2,1)}, bf16[256,1664]{1,0:T(8,128)(2,1)}, bf16[256,512]{1,0:T(8,128)(2,1)}, bf16[256,512]{1,0:T(8,128)(2,1)}, bf16[2...) custom-call(bf16[128,1664]{1,0:T(8,128)(2,1)S(1)} %collective-permut, ...), custom_call_target="tpu_custom_call" | custom-call | flops 3489660928 | bytes 12976128 | tf_op jit(solution)/shard_map/near_rows/pallas_call | solution.py:83
  70.2 1.6 %collective-permute-start.10 = (bf16[128,1664]{1,0:T(8,128)(2,1)S(1)}, bf16[128,1664]{1,0:T(8,128)(2,1)S(1)}, u32[]{:S(2)}, u32[]{:S(2)}) collective-permute-start(bf16[128,1664]{1,0:T(8,128)(2,1)S(1)} %get-tuple-element.67), channel_id=1, source_target_pairs={{0,2},{1,3},{2,4},{3,5},{4,6},{5,7},{6,0},{7,1},{8,10},{9,11},{10,... | collective-permute-start | bytes 1277960 | tf_op jit(solution)/shard_map/ppermute | solution.py:257
  71.7 1.7 %collective-permute-start.11 = (bf16[128,1664]{1,0:T(8,128)(2,1)S(1)}, bf16[128,1664]{1,0:T(8,128)(2,1)S(1)}, u32[]{:S(2)}, u32[]{:S(2)}) collective-permute-start(bf16[128,1664]{1,0:T(8,128)(2,1)S(1)} %get-tuple-element.68), channel_id=1, source_target_pairs={{0,6},{1,7},{2,0},{3,1},{4,2},{5,3},{6,4},{7,5},{8,14},{9,15},{10,... | collective-permute-start | bytes 1277960 | tf_op jit(solution)/shard_map/ppermute | solution.py:257
  73.5 4.0 %far_rows.1 = (bf16[128,1664]{1,0:T(8,128)(2,1)}, bf16[128,1664]{1,0:T(8,128)(2,1)}, bf16[128,512]{1,0:T(8,128)(2,1)}, bf16[128,512]{1,0:T(8,128)(2,1)}, bf16[12...) custom-call(bf16[128,1664]{1,0:T(8,128)(2,1)S(1)} %collective-permut, ...), custom_call_target="tpu_custom_call" | custom-call | flops 1744830464 | bytes 9895936 | tf_op jit(solution)/shard_map/far_rows/pallas_call | solution.py:83
  77.5 0.6 collective-permute-start.8
  78.1 3.0 %collective-permute-start.9 = (bf16[128,1664]{1,0:T(8,128)(2,1)S(1)}, bf16[128,1664]{1,0:T(8,128)(2,1)S(1)}, u32[]{:S(2)}, u32[]{:S(2)}) collective-permute-start(bf16[128,1664]{1,0:T(8,128)(2,1)S(1)} %get-tuple-element.73), channel_id=1, source_target_pairs={{0,6},{1,7},{2,0},{3,1},{4,2},{5,3},{6,4},{7,5},{8,14},{9,15},{10,... | collective-permute-start | bytes 1277960 | tf_op jit(solution)/shard_map/ppermute | solution.py:257
  81.1 2.5 %collective-permute-done.10.refs_2_ = bf16[128,1664]{1,0:T(8,128)(2,1)S(1)} collective-permute-done((bf16[128,1664]{1,0:T(8,128)(2,1)S(1)}, bf16[128,1664]{1,0:T(8,128)(2,1)S(1)}, u32[]{:S(2)}, u32[]{:S(2)}) %collective-permute-start.10) | collective-permute-done | bytes 426016 | tf_op jit(solution)/shard_map/ppermute | solution.py:257
  83.6 0.8 collective-permute-done.11.refs_3_
  84.4 5.4 %weights_b.1 = (bf16[1664,512]{1,0:T(8,128)(2,1)}, bf16[512,1664]{1,0:T(8,128)(2,1)}) custom-call(bf16[256,1664]{1,0:T(8,128)(2,1)} %get-tuple-element.76.refs_0_, bf16[128,1664]{1,0:T(8,128)(2,1)} %get-tuple-element.77.refs_1_, bf16[128,1664]{1,0:T(8,128)(2,1)} %get-tuple-element.78.refs_2_, bf16[256,512]{1,0:T(8,128)(2,1)} %get-tuple-element.79.refs_3_, ...), custom_call_target="tpu_custom_call" | custom-call | flops 1744830464 | bytes 7864320 | tf_op jit(solution)/shard_map/weights_b/pallas_call | solution.py:83
  90.0 1.2 collective-permute-start.12
  91.2 2.1 %collective-permute-start.13 = (bf16[128,1664]{1,0:T(8,128)(2,1)S(1)}, bf16[128,1664]{1,0:T(8,128)(2,1)S(1)}, u32[]{:S(2)}, u32[]{:S(2)}) collective-permute-start(bf16[128,1664]{1,0:T(8,128)(2,1)S(1)} %add_convert_fusion), channel_id=1, source_target_pairs={{0,6},{1,7},{2,0},{3,1},{4,2},{5,3},{6,4},{7,5},{8,14},{9,15},{10,... | collective-permute-start | bytes 1277960 | tf_op jit(solution)/shard_map/ppermute | solution.py:257
  93.3 0.5 collective-permute-start.15
  93.8 5.6 %collective-permute-done.12.refs_1_ = bf16[128,1664]{1,0:T(8,128)(2,1)S(1)} collective-permute-done((bf16[128,1664]{1,0:T(8,128)(2,1)S(1)}, bf16[128,1664]{1,0:T(8,128)(2,1)S(1)}, u32[]{:S(2)}, u32[]{:S(2)}) %collective-permute-start.12) | collective-permute-done | bytes 426016 | tf_op jit(solution)/shard_map/ppermute | solution.py:257
  99.4 1.3 home_sum.1
  100.7 5.9 %all-to-all-start.1 = ((bf16[32,8,1664]{2,1,0:T(8,128)(2,1)}), bf16[32,8,1664]{2,1,0:T(8,128)(2,1)S(1)}, u32[]{:S(2)}, u32[]{:S(2)}) async-start(bf16[32,8,1664]{2,1,0:T(8,128)(2,1)} %bitcast.8), calls=%async_computation.1 | async-start | bytes 1703936 | tf_op jit(solution)/shard_map/all_to_all | solution.py:261
  106.6 1.2 copy-done.4
  107.8 1.5 %copy-done.5 = bf16[1664,512]{1,0:T(8,128)(2,1)S(1)} copy-done((bf16[1664,512]{1,0:T(8,128)(2,1)S(1)}, bf16[1664,512]{1,0:T(8,128)(2,1)}, u32[]{:S(2)}) %copy-start.5) | copy-done | bytes 1703960
  109.3 7.0 %weights_a.1 = (bf16[1664,512]{1,0:T(8,128)(2,1)}, bf16[512,1664]{1,0:T(8,128)(2,1)}) custom-call(bf16[256,1664]{1,0:T(8,128)(2,1)} %get-tuple-element.76.refs_0_, bf16[128,1664]{1,0:T(8,128)(2,1)} %get-tuple-element.77.refs_1_, bf16[128,1664]{1,0:T(8,128)(2,1)} %get-tuple-element.78.refs_2_, bf16[256,512]{1,0:T(8,128)(2,1)} %get-tuple-element.92.refs_3_, ...), custom_call_target="tpu_custom_call" | custom-call | flops 1744830464 | bytes 11272192 | tf_op jit(solution)/shard_map/weights_a/pallas_call | solution.py:83
  116.2 11.3 %all-to-all-done.1 = bf16[32,8,1664]{2,1,0:T(8,128)(2,1)S(1)} async-done(((bf16[32,8,1664]{2,1,0:T(8,128)(2,1)}), bf16[32,8,1664]{2,1,0:T(8,128)(2,1)S(1)}, u32[]{:S(2)}, u32[]{:S(2)}) %all-to-all-start.1) | async-done | bytes 852000 | tf_op jit(solution)/shard_map/all_to_all | solution.py:261
  127.5 2.9 %combine.1 = (bf16[257,1664]{1,0:T(8,128)(2,1)}, bf16[257,1664]{1,0:T(8,128)(2,1)}) custom-call(s32[2,257]{1,0:T(2,128)S(1)} %get-tuple-element.55.refs_0_, f32[2,257]{1,0:T(2,128)S(1)} %bitcast.25, bf16[257,1664]{1,0:T(8,128)(2,1)S(1)} %copy-done.3, f32[1664]{0:T(1024)S(1)} %copy-done.6, bf16[257,1664]{1,0:T(8,128)(2,1)S(1)} %copy-done.2, ...), custom_call_target="tpu_custom_call" | custom-call | flops 437911552 | bytes 4285976 | tf_op jit(solution)/shard_map/combine/pallas_call | solution.py:83
  (30 shorter events, 0.4 us)
Async XLA Ops:
  0.6 39.8 %collective-permute-start = (bf16[1664,512]{1,0:T(8,128)(2,1)}, bf16[1664,512]{1,0:T(8,128)(2,1)S(1)}, u32[]{:S(2)}, u32[]{:S(2)}) collective-permute-start(bf16[1664,512]{1,0:T(8,128)(2,1)} %bitcast.14), channel_id=1, source_target_pairs={{0,1},{1,0},{2,3},{3,2},{4,5},{5,4},{6,7},{7,6},{8,9},{9,8},{10,11... | collective-permute-start | bytes 5111816 | tf_op jit(solution)/shard_map/ppermute | solution.py:257
  0.7 39.7 %collective-permute-start.1 = (bf16[512,1664]{1,0:T(8,128)(2,1)}, bf16[512,1664]{1,0:T(8,128)(2,1)S(1)}, u32[]{:S(2)}, u32[]{:S(2)}) collective-permute-start(bf16[512,1664]{1,0:T(8,128)(2,1)} %bitcast.18), channel_id=1, source_target_pairs={{0,1},{1,0},{2,3},{3,2},{4,5},{5,4},{6,7},{7,6},{8,9},{9,8},{10,11... | collective-permute-start | bytes 5111816 | tf_op jit(solution)/shard_map/ppermute | solution.py:257
  4.5 53.3 %copy-start = (bf16[1,1664,512]{2,1,0:T(8,128)(2,1)S(1)}, bf16[1,1664,512]{2,1,0:T(8,128)(2,1)}, u32[]{:S(2)}) copy-start(bf16[1,1664,512]{2,1,0:T(8,128)(2,1)} %param.20) | copy-start | bytes 5111812
  4.5 53.3 %copy-start.1 = (bf16[1,512,1664]{2,1,0:T(8,128)(2,1)S(1)}, bf16[1,512,1664]{2,1,0:T(8,128)(2,1)}, u32[]{:S(2)}) copy-start(bf16[1,512,1664]{2,1,0:T(8,128)(2,1)} %param.21) | copy-start | bytes 5111812
  40.5 14.0 %collective-permute-start.5 = (bf16[128,1664]{1,0:T(8,128)(2,1)S(1)}, bf16[128,1664]{1,0:T(8,128)(2,1)S(1)}, u32[]{:S(2)}, u32[]{:S(2)}) collective-permute-start(bf16[128,1664]{1,0:T(8,128)(2,1)S(1)} %get-tuple-element.106), channel_id=1, source_target_pairs={{0,2},{1,3},{2,4},{3,5},{4,6},{5,7},{6,0},{7,1},{8,10},{9,11},{10,... | collective-permute-start | bytes 1277960 | tf_op jit(solution)/shard_map/ppermute | solution.py:257
  42.1 12.8 %collective-permute-start.2 = (bf16[128,1664]{1,0:T(8,128)(2,1)S(1)}, bf16[128,1664]{1,0:T(8,128)(2,1)S(1)}, u32[]{:S(2)}, u32[]{:S(2)}) collective-permute-start(bf16[128,1664]{1,0:T(8,128)(2,1)S(1)} %get-tuple-element.107), channel_id=1, source_target_pairs={{0,6},{1,7},{2,0},{3,1},{4,2},{5,3},{6,4},{7,5},{8,14},{9,15},{10,... | collective-permute-start | bytes 1277960 | tf_op jit(solution)/shard_map/ppermute | solution.py:257
  43.8 20.1 %collective-permute-start.3 = (bf16[128,1664]{1,0:T(8,128)(2,1)S(1)}, bf16[128,1664]{1,0:T(8,128)(2,1)S(1)}, u32[]{:S(2)}, u32[]{:S(2)}) collective-permute-start(bf16[128,1664]{1,0:T(8,128)(2,1)S(1)} %get-tuple-element.106), channel_id=1, source_target_pairs={{0,6},{1,7},{2,0},{3,1},{4,2},{5,3},{6,4},{7,5},{8,14},{9,15},{10,... | collective-permute-start | bytes 1277960 | tf_op jit(solution)/shard_map/ppermute | solution.py:257
  45.4 18.6 %collective-permute-start.4 = (bf16[128,1664]{1,0:T(8,128)(2,1)S(1)}, bf16[128,1664]{1,0:T(8,128)(2,1)S(1)}, u32[]{:S(2)}, u32[]{:S(2)}) collective-permute-start(bf16[128,1664]{1,0:T(8,128)(2,1)S(1)} %get-tuple-element.107), channel_id=1, source_target_pairs={{0,2},{1,3},{2,4},{3,5},{4,6},{5,7},{6,0},{7,1},{8,10},{9,11},{10,... | collective-permute-start | bytes 1277960 | tf_op jit(solution)/shard_map/ppermute | solution.py:257
  54.6 18.9 %collective-permute-start.7 = (bf16[128,1664]{1,0:T(8,128)(2,1)S(1)}, bf16[128,1664]{1,0:T(8,128)(2,1)S(1)}, u32[]{:S(2)}, u32[]{:S(2)}) collective-permute-start(bf16[128,1664]{1,0:T(8,128)(2,1)S(1)} %collective-permute-done.5.refs_3_), channel_id=1, source_target_pairs={{0,2},{1,3},{2,4},{3,5},{4,6},{5,7},{6,0},{7,1},{8,10},{9,11},{10,... | collective-permute-start | bytes 1277960 | tf_op jit(solution)/shard_map/ppermute | solution.py:257
  54.8 18.6 %collective-permute-start.6 = (bf16[128,1664]{1,0:T(8,128)(2,1)S(1)}, bf16[128,1664]{1,0:T(8,128)(2,1)S(1)}, u32[]{:S(2)}, u32[]{:S(2)}) collective-permute-start(bf16[128,1664]{1,0:T(8,128)(2,1)S(1)} %collective-permute-done.2.refs_0_), channel_id=1, source_target_pairs={{0,6},{1,7},{2,0},{3,1},{4,2},{5,3},{6,4},{7,5},{8,14},{9,15},{10,... | collective-permute-start | bytes 1277960 | tf_op jit(solution)/shard_map/ppermute | solution.py:257
  70.2 13.4 %collective-permute-start.10 = (bf16[128,1664]{1,0:T(8,128)(2,1)S(1)}, bf16[128,1664]{1,0:T(8,128)(2,1)S(1)}, u32[]{:S(2)}, u32[]{:S(2)}) collective-permute-start(bf16[128,1664]{1,0:T(8,128)(2,1)S(1)} %get-tuple-element.67), channel_id=1, source_target_pairs={{0,2},{1,3},{2,4},{3,5},{4,6},{5,7},{6,0},{7,1},{8,10},{9,11},{10,... | collective-permute-start | bytes 1277960 | tf_op jit(solution)/shard_map/ppermute | solution.py:257
  71.7 12.6 %collective-permute-start.11 = (bf16[128,1664]{1,0:T(8,128)(2,1)S(1)}, bf16[128,1664]{1,0:T(8,128)(2,1)S(1)}, u32[]{:S(2)}, u32[]{:S(2)}) collective-permute-start(bf16[128,1664]{1,0:T(8,128)(2,1)S(1)} %get-tuple-element.68), channel_id=1, source_target_pairs={{0,6},{1,7},{2,0},{3,1},{4,2},{5,3},{6,4},{7,5},{8,14},{9,15},{10,... | collective-permute-start | bytes 1277960 | tf_op jit(solution)/shard_map/ppermute | solution.py:257
  77.5 12.2 %collective-permute-start.8 = (bf16[128,1664]{1,0:T(8,128)(2,1)S(1)}, bf16[128,1664]{1,0:T(8,128)(2,1)S(1)}, u32[]{:S(2)}, u32[]{:S(2)}) collective-permute-start(bf16[128,1664]{1,0:T(8,128)(2,1)S(1)} %get-tuple-element.71), channel_id=1, source_target_pairs={{0,2},{1,3},{2,4},{3,5},{4,6},{5,7},{6,0},{7,1},{8,10},{9,11},{10,... | collective-permute-start | bytes 1277960 | tf_op jit(solution)/shard_map/ppermute | solution.py:257
  78.1 11.8 %collective-permute-start.9 = (bf16[128,1664]{1,0:T(8,128)(2,1)S(1)}, bf16[128,1664]{1,0:T(8,128)(2,1)S(1)}, u32[]{:S(2)}, u32[]{:S(2)}) collective-permute-start(bf16[128,1664]{1,0:T(8,128)(2,1)S(1)} %get-tuple-element.73), channel_id=1, source_target_pairs={{0,6},{1,7},{2,0},{3,1},{4,2},{5,3},{6,4},{7,5},{8,14},{9,15},{10,... | collective-permute-start | bytes 1277960 | tf_op jit(solution)/shard_map/ppermute | solution.py:257
  90.0 9.4 %collective-permute-start.12 = (bf16[128,1664]{1,0:T(8,128)(2,1)S(1)}, bf16[128,1664]{1,0:T(8,128)(2,1)S(1)}, u32[]{:S(2)}, u32[]{:S(2)}) collective-permute-start(bf16[128,1664]{1,0:T(8,128)(2,1)S(1)} %add_convert_fusion.1), channel_id=1, source_target_pairs={{0,2},{1,3},{2,4},{3,5},{4,6},{5,7},{6,0},{7,1},{8,10},{9,11},{10,... | collective-permute-start | bytes 1277960 | tf_op jit(solution)/shard_map/ppermute | solution.py:257
  91.2 8.2 %collective-permute-start.13 = (bf16[128,1664]{1,0:T(8,128)(2,1)S(1)}, bf16[128,1664]{1,0:T(8,128)(2,1)S(1)}, u32[]{:S(2)}, u32[]{:S(2)}) collective-permute-start(bf16[128,1664]{1,0:T(8,128)(2,1)S(1)} %add_convert_fusion), channel_id=1, source_target_pairs={{0,6},{1,7},{2,0},{3,1},{4,2},{5,3},{6,4},{7,5},{8,14},{9,15},{10,... | collective-permute-start | bytes 1277960 | tf_op jit(solution)/shard_map/ppermute | solution.py:257
  93.3 13.3 %collective-permute-start.14 = (bf16[1664,512]{1,0:T(8,128)(2,1)}, bf16[1664,512]{1,0:T(8,128)(2,1)S(1)}, u32[]{:S(2)}, u32[]{:S(2)}) collective-permute-start(bf16[1664,512]{1,0:T(8,128)(2,1)} %get-tuple-element.98), channel_id=1, source_target_pairs={{0,1},{1,0},{2,3},{3,2},{4,5},{5,4},{6,7},{7,6},{8,9},{9,8},{10,11... | collective-permute-start | bytes 5111816 | tf_op jit(solution)/shard_map/ppermute | solution.py:257
  93.3 14.5 %collective-permute-start.15 = (bf16[512,1664]{1,0:T(8,128)(2,1)}, bf16[512,1664]{1,0:T(8,128)(2,1)}, u32[]{:S(2)}, u32[]{:S(2)}) collective-permute-start(bf16[512,1664]{1,0:T(8,128)(2,1)} %get-tuple-element.99), channel_id=1, source_target_pairs={{0,1},{1,0},{2,3},{3,2},{4,5},{5,4},{6,7},{7,6},{8,9},{9,8},{10,11... | collective-permute-start | bytes 5111816 | tf_op jit(solution)/shard_map/ppermute | solution.py:257
  100.7 26.8 %all-to-all-start.1 = ((bf16[32,8,1664]{2,1,0:T(8,128)(2,1)}), bf16[32,8,1664]{2,1,0:T(8,128)(2,1)S(1)}, u32[]{:S(2)}, u32[]{:S(2)}) async-start(bf16[32,8,1664]{2,1,0:T(8,128)(2,1)} %bitcast.8), calls=%async_computation.1 | async-start | bytes 1703936 | tf_op jit(solution)/shard_map/all_to_all | solution.py:261
  106.6 1.2 copy-start.4
  107.8 1.5 %copy-start.5 = (bf16[1664,512]{1,0:T(8,128)(2,1)S(1)}, bf16[1664,512]{1,0:T(8,128)(2,1)}, u32[]{:S(2)}) copy-start(bf16[1664,512]{1,0:T(8,128)(2,1)} %copy-done.4) | copy-start | bytes 5111812
  109.3 18.3 %copy-start.2 = (bf16[257,1664]{1,0:T(8,128)(2,1)S(1)}, bf16[257,1664]{1,0:T(8,128)(2,1)}, u32[]{:S(2)}) copy-start(bf16[257,1664]{1,0:T(8,128)(2,1)} %refs_4_.1) | copy-start | bytes 2565892
  109.3 18.3 %copy-start.3 = (bf16[257,1664]{1,0:T(8,128)(2,1)S(1)}, bf16[257,1664]{1,0:T(8,128)(2,1)}, u32[]{:S(2)}) copy-start(bf16[257,1664]{1,0:T(8,128)(2,1)} %refs_2_.1) | copy-start | bytes 2565892
  109.3 18.3 %copy-start.6 = (f32[1664]{0:T(1024)S(1)}, f32[1664]{0:T(1024)}, u32[]{:S(2)}) copy-start(f32[1664]{0:T(1024)} %refs_3_.1) | copy-start | bytes 19972
  109.3 18.3 %copy-start.7 = (f32[257,2]{0,1:T(2,128)S(1)}, f32[257,2]{0,1:T(2,128)}, u32[]{:S(2)}) copy-start(f32[257,2]{0,1:T(2,128)} %param.13) | copy-start | bytes 6172

commit v3 on v1

--- a/solution.py
+++ b/solution.py
@@ -21,21 +21,29 @@
 
 def call(body, outs, ins, scalars=(), here=(), keep=(), flops=0, name=None):
     n_in, n_out, n_s = len(ins), len(outs), len(scalars)
+    ins = [list(a) if isinstance(a, (list, tuple)) else [a] for a in ins]
+    flat_in = [a for group in ins for a in group]
+    first = [sum(len(g) for g in ins[:i]) for i in range(n_in)]
     far_in = [i for i in range(n_in) if i not in here]
     far_out = [i for i in range(n_out) if i not in keep]
 
     def kernel(*refs):
         words, refs = refs[:n_s], refs[n_s:]
-        source, refs = refs[:n_in], refs[n_in:]
+        source, refs = refs[: len(flat_in)], refs[len(flat_in) :]
         sink, refs = refs[:n_out], refs[n_out:]
         held, refs = dict(zip(far_in, refs)), refs[len(far_in) :]
         made, refs = dict(zip(far_out, refs)), refs[len(far_out) :]
         in_sem, out_sem, word_sem, *smem = refs
         word_copies = [pltpu.make_async_copy(a, b, word_sem.at[k]) for k, (a, b) in enumerate(zip(words, smem))]
-        for c in word_copies:
-            c.start()
-        copies = {i: pltpu.make_async_copy(source[i], held[i], in_sem.at[k]) for k, i in enumerate(far_in)}
-        for c in copies.values():
+        copies = {}
+        for i in far_in:
+            at, copies[i] = 0, []
+            for k in range(first[i], first[i] + len(ins[i])):
+                n = flat_in[k].shape[0]
+                target = held[i] if len(ins[i]) == 1 else held[i].at[pl.ds(at, n)]
+                copies[i].append(pltpu.make_async_copy(source[k], target, in_sem.at[k]))
+                at += n
+        for c in word_copies + [c for group in copies.values() for c in group]:
             c.start()
         for c in word_copies:
             c.wait()
@@ -43,10 +51,11 @@
 
         def load(i):
             if i not in copies:
-                return source[i]
+                return source[first[i]]
             if i not in waited:
                 waited.add(i)
-                copies[i].wait()
+                for c in copies[i]:
+                    c.wait()
             return held[i]
 
         def store(i):
@@ -59,24 +68,28 @@
         for c in sent:
             c.wait()
 
-    moved = sum(a.size * a.dtype.itemsize for a in list(outs) + list(ins))
-    buffers = [pltpu.VMEM(ins[i].shape, ins[i].dtype) for i in far_in]
+    moved = sum(a.size * a.dtype.itemsize for a in list(outs) + flat_in)
+    buffers = [pltpu.VMEM((sum(a.shape[0] for a in ins[i]),) + ins[i][0].shape[1:], ins[i][0].dtype) for i in far_in]
     buffers += [pltpu.VMEM(outs[i].shape, outs[i].dtype) for i in far_out]
-    sems = [pltpu.SemaphoreType.DMA((max(1, len(k)),)) for k in (far_in, far_out, scalars)]
-    words = [pltpu.SMEM(a.shape, a.dtype) for a in scalars]
+    sems = [pltpu.SemaphoreType.DMA((max(1, k),)) for k in (len(flat_in), len(far_out), n_s)]
+    smem_words = [pltpu.SMEM(a.shape, a.dtype) for a in scalars]
     scalars = [pltpu.with_memory_space_constraint(a, pltpu.HBM) for a in scalars]
-    ins = [a if i in here else pltpu.with_memory_space_constraint(a, pltpu.HBM) for i, a in enumerate(ins)]
+    given, specs = [], [HBM] * n_s
+    for i, group in enumerate(ins):
+        for a in group:
+            given.append(a if i in here else pltpu.with_memory_space_constraint(a, pltpu.HBM))
+            specs.append(VMEM if i in here else HBM)
     outs = [o if i in keep else pltpu.HBM(o.shape, o.dtype) for i, o in enumerate(outs)]
     return pl.pallas_call(
         kernel,
         out_shape=outs,
-        in_specs=[HBM] * n_s + [VMEM if i in here else HBM for i in range(n_in)],
+        in_specs=specs,
         out_specs=[VMEM if i in keep else HBM for i in range(n_out)],
-        scratch_shapes=buffers + sems + words,
+        scratch_shapes=buffers + sems + smem_words,
         compiler_params=pltpu.CompilerParams(vmem_limit_bytes=28 * MIB),
         cost_estimate=pl.CostEstimate(flops=flops, bytes_accessed=moved, transcendentals=0),
         name=name,
-    )(*scalars, *ins)
+    )(*scalars, *given)
 
 
 def after(values, *others):
@@ -172,23 +185,17 @@
         at += size
 
 
-def tall_product(load, first):
-    total = None
-    for i in (first, first + 2, first + 4):
-        term = lax.dot_general(load(i)[...], load(i + 1)[...], TN, preferred_element_type=F32)
-        total = term if total is None else total + term
-    return total
-
-
 def weight_grads(load, made, store, smem):
     for k in range(2):
-        made[k][...] = tall_product(load, 6 * k).astype(BF16)
+        total = lax.dot_general(load(2 * k)[...], load(2 * k + 1)[...], TN, preferred_element_type=F32)
+        made[k][...] = total.astype(BF16)
         store(k)
 
 
 def weight_sums(load, made, store, smem):
     for k in range(2):
-        made[k][...] = (tall_product(load, 6 * k) + load(12 + k)[...].astype(F32)).astype(BF16)
+        total = lax.dot_general(load(2 * k)[...], load(2 * k + 1)[...], TN, preferred_element_type=F32)
+        made[k][...] = (total + load(4 + k)[...].astype(F32)).astype(BF16)
         store(k)
 
 
@@ -259,8 +266,7 @@
         flops=2 * small,
         name="dispatch",
     )
-    in_b, out_b = after((in_a, out_a), target)
-    in_b, out_b = send(in_b, sibling), send(out_b, sibling)
+    in_b, out_b = send(in_a, sibling), send(out_a, sibling)
     rows, in_b, out_b = lax.optimization_barrier((exchange(rows), in_b, out_b))
     top, bottom = rows[:half], rows[half:]
     near = send(top, left), send(bottom, left), send(top, right), send(bottom, right)
@@ -293,14 +299,12 @@
     far_top, far_bottom = send(far_top, right), send(far_bottom, left)
     first, second = sds(in_a.shape, BF16), sds(out_a.shape, BF16)
     flops = 4 * n_rows * features * hidden
+    x_near, grad_b = after((x_near, grad_b), right_bottom, left_top)
+    x_all, g_all = [x_near, x_far, x_own], [g_near, g_far, g_own]
+    act_b, grad_b = [act_b, far_act_b, own_act_b], [grad_b, far_grad_b, own_grad_b]
+    act_a, grad_a = [act_a, far_act_a, own_act_a], [grad_a, far_grad_a, own_grad_a]
     first_b, second_b = call(
-        weight_grads,
-        [first, second],
-        after([x_near, grad_b], right_bottom, left_top)
-        + [x_far, far_grad_b, x_own, own_grad_b, act_b, g_near, far_act_b, g_far, own_act_b, g_own],
-        keep=range(2),
-        flops=flops,
-        name="weights_b",
+        weight_grads, [first, second], [x_all, grad_b, act_b, g_all], keep=range(2), flops=flops, name="weights_b"
     )
     right_top, left_bottom, first_b, second_b = lax.optimization_barrier(
         (add(right_top, far_top), add(left_bottom, far_bottom), first_b, second_b)
@@ -313,9 +317,8 @@
     grad_first, grad_second = call(
         weight_sums,
         [first, second],
-        [x_near, grad_a, x_far, far_grad_a, x_own, own_grad_a]
-        + [act_a, g_near, far_act_a, g_far, own_act_a, g_own, more_first, more_second],
-        here=(12, 13),
+        [x_all, grad_a, act_a, g_all, more_first, more_second],
+        here=(4, 5),
         flops=flops,
         name="weights_a",
     )

time: 131 us -> 131 us (level)
  Pallas kernels: 33.3 us -> 31.6 us
    pallas_call x8, Pallas kernels: 33.3 us -> 31.6 us  [call(): pl.pallas_call(kernel, out_shape=outs, in_specs=specs, out_specs=[VMEM if...]
  transfers between devices with their start and end apart: 17 -> 17, of which waited for: 8 -> 8; matrix products, arithmetic and copies ran while one was open for 0% -> 0% of each run, Pallas kernels for 21% -> 22%
where the time goes in v3:
time: 131 us; the launch traced here: 130 us
  blocking collectives  35.9 us (27%)
  waiting for transfers between devices  32 us (24%)
  Pallas kernels  31.6 us (24%)
  starting transfers between devices  26.5 us (20%)
  local copies, waits for them, and re-layouts  2.96 us (2%)
    all_to_all x1, blocking collectives, exchange(): return lax.all_to_all(rows, 'expert', 0, 0, tiled=True)  35.9 us
    pallas_call x8, Pallas kernels, call(): pl.pallas_call(kernel, out_shape=outs, in_specs=specs, out_specs=[VMEM if...  31.6 us
    ppermute x16, waiting for transfers between devices, send(): return lax.ppermute(array, 'dp', pairs)  20.9 us
    ppermute x16, starting transfers between devices, send(): return lax.ppermute(array, 'dp', pairs)  19.6 us
    all_to_all x1, waiting for transfers between devices, exchange(): return lax.all_to_all(rows, 'expert', 0, 0, tiled=True)  11.1 us
    all_to_all x1, starting transfers between devices, exchange(): return lax.all_to_all(rows, 'expert', 0, 0, tiled=True)  6.86 us
    unnamed x16, local copies, waits for them, and re-layouts  2.66 us
  transfers between devices with their start and end apart: 17, of which 8 were waited for; matrix products, arithmetic and copies ran while one was open for 0% of the time, Pallas kernels for 22%

profile of v3, /device:TPU:8, one launch (start us, length us, event | category | flops | bytes accessed | tf_op | source)
XLA Modules:
  0.0 130.3 jit_solution(14061818119253699234)
XLA Ops:
  0.7 0.5 collective-permute-start.1
  1.2 2.8 %dispatch.1 = (bf16[32,2,4,1664]{3,2,1,0:T(4,128)(2,1)S(1)}, s32[2,257]{1,0:T(2,128)S(1)}, f32[257,2]{1,0:T(8,128)S(1)}) custom-call(s32[1,32]{1,0:T(1,128)} %refs_0_.1, s32[2,257]{1,0:T(2,128)} %bitcast.18, s32[2,257]{1,0:T(2,128)} %bitcast.19, s32[2,257]{1,0:T(2,128)} %bitcast.20, f32[2,257]{1,0:T(2,128)} %bitcast.16, bf16[257,1664]{1,0:T(8,128)(2,1)} %refs_4_.1, ...), custom_call_target="tpu_custom_call" | custom-call | flops 218955776 | bytes 2588208 | tf_op jit(solution)/shard_map/dispatch/pallas_call | solution.py:83
  4.1 35.9 %all_to_all.10.refs_0_ = bf16[32,2,4,1664]{3,2,1,0:T(4,128)(2,1)S(1)} all-to-all(bf16[32,2,4,1664]{3,2,1,0:T(4,128)(2,1)S(1)} %get-tuple-element.56), channel_id=1, replica_groups=mesh['expert'=32,'dp'=8] {'expert'}, dimensions={0} | all-to-all | bytes 1703936 | tf_op jit(solution)/shard_map/all_to_all | solution.py:251
  40.3 1.6 %collective-permute-start.5 = (bf16[16,2,4,1664]{3,2,1,0:T(4,128)(2,1)S(1)}, bf16[16,2,4,1664]{3,2,1,0:T(4,128)(2,1)S(1)}, u32[]{:S(2)}, u32[]{:S(2)}) collective-permute-start(bf16[16,2,4,1664]{3,2,1,0:T(4,128)(2,1)S(1)} %get-tuple-element.106), channel_id=1, source_target_pairs={{0,2},{1,3},{2,4},{3,5},{4,6},{5,7},{6,0},{7,1},{8,10},{9,11},{10,... | collective-permute-start | bytes 1277960 | tf_op jit(solution)/shard_map/ppermute | solution.py:248
  41.8 1.7 %collective-permute-start.2 = (bf16[16,2,4,1664]{3,2,1,0:T(4,128)(2,1)S(1)}, bf16[16,2,4,1664]{3,2,1,0:T(4,128)(2,1)S(1)}, u32[]{:S(2)}, u32[]{:S(2)}) collective-permute-start(bf16[16,2,4,1664]{3,2,1,0:T(4,128)(2,1)S(1)} %get-tuple-element.107), channel_id=1, source_target_pairs={{0,6},{1,7},{2,0},{3,1},{4,2},{5,3},{6,4},{7,5},{8,14},{9,15},{10,... | collective-permute-start | bytes 1277960 | tf_op jit(solution)/shard_map/ppermute | solution.py:248
  43.6 1.6 %collective-permute-start.3 = (bf16[16,2,4,1664]{3,2,1,0:T(4,128)(2,1)S(1)}, bf16[16,2,4,1664]{3,2,1,0:T(4,128)(2,1)S(1)}, u32[]{:S(2)}, u32[]{:S(2)}) collective-permute-start(bf16[16,2,4,1664]{3,2,1,0:T(4,128)(2,1)S(1)} %get-tuple-element.106), channel_id=1, source_target_pairs={{0,6},{1,7},{2,0},{3,1},{4,2},{5,3},{6,4},{7,5},{8,14},{9,15},{10,... | collective-permute-start | bytes 1277960 | tf_op jit(solution)/shard_map/ppermute | solution.py:248
  45.1 0.5 collective-permute-start.4
  45.6 8.7 %collective-permute-done.5.refs_3_ = bf16[16,2,4,1664]{3,2,1,0:T(4,128)(2,1)S(1)} collective-permute-done((bf16[16,2,4,1664]{3,2,1,0:T(4,128)(2,1)S(1)}, bf16[16,2,4,1664]{3,2,1,0:T(4,128)(2,1)S(1)}, u32[]{:S(2)}, u32[]{:S(2)}) %collective-permute-start.5) | collective-permute-done | bytes 426016 | tf_op jit(solution)/shard_map/ppermute | solution.py:248
  54.6 3.0 %collective-permute-start.6 = (bf16[16,2,4,1664]{3,2,1,0:T(4,128)(2,1)S(1)}, bf16[16,2,4,1664]{3,2,1,0:T(4,128)(2,1)S(1)}, u32[]{:S(2)}, u32[]{:S(2)}) collective-permute-start(bf16[16,2,4,1664]{3,2,1,0:T(4,128)(2,1)S(1)} %collective-permute-done.2.refs_0_), channel_id=1, source_target_pairs={{0,6},{1,7},{2,0},{3,1},{4,2},{5,3},{6,4},{7,5},{8,14},{9,15},{10,... | collective-permute-start | bytes 1277960 | tf_op jit(solution)/shard_map/ppermute | solution.py:248
  57.5 3.2 %own_rows.1 = (bf16[128,1664]{1,0:T(8,128)(2,1)}, bf16[128,1664]{1,0:T(8,128)(2,1)}, bf16[128,512]{1,0:T(8,128)(2,1)}, bf16[128,512]{1,0:T(8,128)(2,1)}, bf16[12...) custom-call(bf16[32,2,4,1664]{3,2,1,0:T(4,128)(2,1)S(1)} %all_to_all.10.refs_0_, ...), custom_call_target="tpu_custom_call" | custom-call | flops 1744830464 | bytes 10747904 | tf_op jit(solution)/shard_map/own_rows/pallas_call | solution.py:83
  60.7 3.0 %collective-permute-done.3.refs_1_ = bf16[16,2,4,1664]{3,2,1,0:T(4,128)(2,1)S(1)} collective-permute-done((bf16[16,2,4,1664]{3,2,1,0:T(4,128)(2,1)S(1)}, bf16[16,2,4,1664]{3,2,1,0:T(4,128)(2,1)S(1)}, u32[]{:S(2)}, u32[]{:S(2)}) %collective-permute-start.3) | collective-permute-done | bytes 426016 | tf_op jit(solution)/shard_map/ppermute | solution.py:248
  63.7 5.0 %near_rows.1 = (bf16[256,1664]{1,0:T(8,128)(2,1)}, bf16[256,1664]{1,0:T(8,128)(2,1)}, bf16[256,512]{1,0:T(8,128)(2,1)}, bf16[256,512]{1,0:T(8,128)(2,1)}, bf16[2...) custom-call(bf16[16,2,4,1664]{3,2,1,0:T(4,128)(2,1)S(1)} %collective, ...), custom_call_target="tpu_custom_call" | custom-call | flops 3489660928 | bytes 12976128 | tf_op jit(solution)/shard_map/near_rows/pallas_call | solution.py:83
  68.7 1.6 %collective-permute-start.10 = (bf16[16,2,4,1664]{3,2,1,0:T(4,128)(2,1)S(1)}, bf16[16,2,4,1664]{3,2,1,0:T(4,128)(2,1)S(1)}, u32[]{:S(2)}, u32[]{:S(2)}) collective-permute-start(bf16[16,2,4,1664]{3,2,1,0:T(4,128)(2,1)S(1)} %get-tuple-element.67), channel_id=1, source_target_pairs={{0,2},{1,3},{2,4},{3,5},{4,6},{5,7},{6,0},{7,1},{8,10},{9,11},{10,... | collective-permute-start | bytes 1277960 | tf_op jit(solution)/shard_map/ppermute | solution.py:248
  70.3 1.7 %collective-permute-start.11 = (bf16[16,2,4,1664]{3,2,1,0:T(4,128)(2,1)S(1)}, bf16[16,2,4,1664]{3,2,1,0:T(4,128)(2,1)S(1)}, u32[]{:S(2)}, u32[]{:S(2)}) collective-permute-start(bf16[16,2,4,1664]{3,2,1,0:T(4,128)(2,1)S(1)} %get-tuple-element.68), channel_id=1, source_target_pairs={{0,6},{1,7},{2,0},{3,1},{4,2},{5,3},{6,4},{7,5},{8,14},{9,15},{10,... | collective-permute-start | bytes 1277960 | tf_op jit(solution)/shard_map/ppermute | solution.py:248
  72.0 0.6 collective-permute-done.7.refs_1_
  72.8 4.1 %far_rows.1 = (bf16[128,1664]{1,0:T(8,128)(2,1)}, bf16[128,1664]{1,0:T(8,128)(2,1)}, bf16[128,512]{1,0:T(8,128)(2,1)}, bf16[128,512]{1,0:T(8,128)(2,1)}, bf16[12...) custom-call(bf16[16,2,4,1664]{3,2,1,0:T(4,128)(2,1)S(1)} %collective, ...), custom_call_target="tpu_custom_call" | custom-call | flops 1744830464 | bytes 9895936 | tf_op jit(solution)/shard_map/far_rows/pallas_call | solution.py:83
  76.9 1.6 %collective-permute-start.8 = (bf16[16,2,4,1664]{3,2,1,0:T(4,128)(2,1)S(1)}, bf16[16,2,4,1664]{3,2,1,0:T(4,128)(2,1)S(1)}, u32[]{:S(2)}, u32[]{:S(2)}) collective-permute-start(bf16[16,2,4,1664]{3,2,1,0:T(4,128)(2,1)S(1)} %get-tuple-element.71), channel_id=1, source_target_pairs={{0,2},{1,3},{2,4},{3,5},{4,6},{5,7},{6,0},{7,1},{8,10},{9,11},{10,... | collective-permute-start | bytes 1277960 | tf_op jit(solution)/shard_map/ppermute | solution.py:248
  78.5 1.7 %collective-permute-start.9 = (bf16[16,2,4,1664]{3,2,1,0:T(4,128)(2,1)S(1)}, bf16[16,2,4,1664]{3,2,1,0:T(4,128)(2,1)S(1)}, u32[]{:S(2)}, u32[]{:S(2)}) collective-permute-start(bf16[16,2,4,1664]{3,2,1,0:T(4,128)(2,1)S(1)} %get-tuple-element.73), channel_id=1, source_target_pairs={{0,6},{1,7},{2,0},{3,1},{4,2},{5,3},{6,4},{7,5},{8,14},{9,15},{10,... | collective-permute-start | bytes 1277960 | tf_op jit(solution)/shard_map/ppermute | solution.py:248
  80.3 2.4 %collective-permute-done.10.refs_2_ = bf16[16,2,4,1664]{3,2,1,0:T(4,128)(2,1)S(1)} collective-permute-done((bf16[16,2,4,1664]{3,2,1,0:T(4,128)(2,1)S(1)}, bf16[16,2,4,1664]{3,2,1,0:T(4,128)(2,1)S(1)}, u32[]{:S(2)}, u32[]{:S(2)}) %collective-permute-start.10) | collective-permute-done | bytes 426016 | tf_op jit(solution)/shard_map/ppermute | solution.py:248
  82.7 0.3 collective-permute-done.11.refs_3_
  83.0 5.4 %weights_b.1 = (bf16[1664,512]{1,0:T(8,128)(2,1)}, bf16[512,1664]{1,0:T(8,128)(2,1)}) custom-call(bf16[256,1664]{1,0:T(8,128)(2,1)} %get-tuple-element.76.refs_0_, bf16[128,1664]{1,0:T(8,128)(2,1)} %get-tuple-element.77.refs_1_, bf16[128,1664]{1,0:T(8,128)(2,1)} %get-tuple-element.78.refs_2_, bf16[256,512]{1,0:T(8,128)(2,1)} %get-tuple-element.79.refs_3_, ...), custom_call_target="tpu_custom_call" | custom-call | flops 1744830464 | bytes 7864320 | tf_op jit(solution)/shard_map/weights_b/pallas_call | solution.py:83
  88.8 1.3 %collective-permute-start.12 = (bf16[16,2,4,1664]{3,2,1,0:T(4,128)(2,1)S(1)}, bf16[16,2,4,1664]{3,2,1,0:T(4,128)(2,1)S(1)}, u32[]{:S(2)}, u32[]{:S(2)}) collective-permute-start(bf16[16,2,4,1664]{3,2,1,0:T(4,128)(2,1)S(1)} %add_convert_fusion.1), channel_id=1, source_target_pairs={{0,2},{1,3},{2,4},{3,5},{4,6},{5,7},{6,0},{7,1},{8,10},{9,11},{10,... | collective-permute-start | bytes 1277960 | tf_op jit(solution)/shard_map/ppermute | solution.py:248
  90.1 2.0 %collective-permute-start.13 = (bf16[16,2,4,1664]{3,2,1,0:T(4,128)(2,1)S(1)}, bf16[16,2,4,1664]{3,2,1,0:T(4,128)(2,1)S(1)}, u32[]{:S(2)}, u32[]{:S(2)}) collective-permute-start(bf16[16,2,4,1664]{3,2,1,0:T(4,128)(2,1)S(1)} %add_convert_fusion), channel_id=1, source_target_pairs={{0,6},{1,7},{2,0},{3,1},{4,2},{5,3},{6,4},{7,5},{8,14},{9,15},{10,... | collective-permute-start | bytes 1277960 | tf_op jit(solution)/shard_map/ppermute | solution.py:248
  92.1 0.5 collective-permute-start.15
  92.6 5.6 %collective-permute-done.12.refs_1_ = bf16[16,2,4,1664]{3,2,1,0:T(4,128)(2,1)S(1)} collective-permute-done((bf16[16,2,4,1664]{3,2,1,0:T(4,128)(2,1)S(1)}, bf16[16,2,4,1664]{3,2,1,0:T(4,128)(2,1)S(1)}, u32[]{:S(2)}, u32[]{:S(2)}) %collective-permute-start.12) | collective-permute-done | bytes 426016 | tf_op jit(solution)/shard_map/ppermute | solution.py:248
  98.3 1.4 %home_sum.1 = bf16[32,2,4,1664]{3,2,1,0:T(4,128)(2,1)} custom-call(f32[32,2,4,1664]{3,2,1,0:T(4,128)S(1)} %get-tuple-element.61.refs_0_, bf16[16,2,4,1664]{3,2,1,0:T(4,128)(2,1)S(1)} %collective-permute-done.12.refs_1_, bf16[16,2,4,1664]{3,2,1,0:T(4,128)(2,1)S(1)} %collective-permute-done.10.refs_2_, ...), custom_call_target="tpu_custom_call" | custom-call | bytes 4259840 | tf_op jit(solution)/shard_map/home_sum/pallas_call | solution.py:83
  99.7 6.9 %all-to-all-start.1 = ((bf16[32,2,4,1664]{3,2,1,0:T(4,128)(2,1)}), bf16[32,2,4,1664]{3,2,1,0:T(4,128)(2,1)S(1)}, u32[]{:S(2)}, u32[]{:S(2)}) async-start(bf16[32,2,4,1664]{3,2,1,0:T(4,128)(2,1)} %home_sum.1), calls=%async_computation.1 | async-start | bytes 1703936 | tf_op jit(solution)/shard_map/all_to_all | solution.py:251
  106.6 1.2 copy-done.4
  107.7 1.5 %copy-done.5 = bf16[1664,512]{1,0:T(8,128)(2,1)S(1)} copy-done((bf16[1664,512]{1,0:T(8,128)(2,1)S(1)}, bf16[1664,512]{1,0:T(8,128)(2,1)}, u32[]{:S(2)}) %copy-start.5) | copy-done | bytes 1703960
  109.2 7.0 %weights_a.1 = (bf16[1664,512]{1,0:T(8,128)(2,1)}, bf16[512,1664]{1,0:T(8,128)(2,1)}) custom-call(bf16[256,1664]{1,0:T(8,128)(2,1)} %get-tuple-element.76.refs_0_, bf16[128,1664]{1,0:T(8,128)(2,1)} %get-tuple-element.77.refs_1_, bf16[128,1664]{1,0:T(8,128)(2,1)} %get-tuple-element.78.refs_2_, bf16[256,512]{1,0:T(8,128)(2,1)} %get-tuple-element.92.refs_3_, ...), custom_call_target="tpu_custom_call" | custom-call | flops 1744830464 | bytes 11272192 | tf_op jit(solution)/shard_map/weights_a/pallas_call | solution.py:83
  116.2 11.1 %all-to-all-done.1.refs_5_ = bf16[32,2,4,1664]{3,2,1,0:T(4,128)(2,1)S(1)} async-done(((bf16[32,2,4,1664]{3,2,1,0:T(4,128)(2,1)}), bf16[32,2,4,1664]{3,2,1,0:T(4,128)(2,1)S(1)}, u32[]{:S(2)}, u32[]{:S(2)}) %all-to-all-start.1) | async-done | bytes 852000 | tf_op jit(solution)/shard_map/all_to_all | solution.py:251
  127.3 2.8 %combine.1 = (bf16[257,1664]{1,0:T(8,128)(2,1)}, bf16[257,1664]{1,0:T(8,128)(2,1)}) custom-call(s32[2,257]{1,0:T(2,128)S(1)} %get-tuple-element.55.refs_0_, f32[2,257]{1,0:T(2,128)S(1)} %bitcast.17, bf16[257,1664]{1,0:T(8,128)(2,1)S(1)} %copy-done.3, f32[1664]{0:T(1024)S(1)} %copy-done.6, bf16[257,1664]{1,0:T(8,128)(2,1)S(1)} %copy-done.2, ...), custom_call_target="tpu_custom_call" | custom-call | flops 437911552 | bytes 4285976 | tf_op jit(solution)/shard_map/combine/pallas_call | solution.py:83
  (30 shorter events, 1.5 us)
Async XLA Ops:
  0.6 39.3 %collective-permute-start = (bf16[1664,512]{1,0:T(8,128)(2,1)}, bf16[1664,512]{1,0:T(8,128)(2,1)S(1)}, u32[]{:S(2)}, u32[]{:S(2)}) collective-permute-start(bf16[1664,512]{1,0:T(8,128)(2,1)} %bitcast.8), channel_id=1, source_target_pairs={{0,1},{1,0},{2,3},{3,2},{4,5},{5,4},{6,7},{7,6},{8,9},{9,8},{10,11... | collective-permute-start | bytes 5111816 | tf_op jit(solution)/shard_map/ppermute | solution.py:248
  0.7 39.2 %collective-permute-start.1 = (bf16[512,1664]{1,0:T(8,128)(2,1)}, bf16[512,1664]{1,0:T(8,128)(2,1)S(1)}, u32[]{:S(2)}, u32[]{:S(2)}) collective-permute-start(bf16[512,1664]{1,0:T(8,128)(2,1)} %bitcast.12), channel_id=1, source_target_pairs={{0,1},{1,0},{2,3},{3,2},{4,5},{5,4},{6,7},{7,6},{8,9},{9,8},{10,11... | collective-permute-start | bytes 5111816 | tf_op jit(solution)/shard_map/ppermute | solution.py:248
  4.0 53.5 %copy-start = (bf16[1,1664,512]{2,1,0:T(8,128)(2,1)S(1)}, bf16[1,1664,512]{2,1,0:T(8,128)(2,1)}, u32[]{:S(2)}) copy-start(bf16[1,1664,512]{2,1,0:T(8,128)(2,1)} %param.20) | copy-start | bytes 5111812
  4.1 53.5 %copy-start.1 = (bf16[1,512,1664]{2,1,0:T(8,128)(2,1)S(1)}, bf16[1,512,1664]{2,1,0:T(8,128)(2,1)}, u32[]{:S(2)}) copy-start(bf16[1,512,1664]{2,1,0:T(8,128)(2,1)} %param.21) | copy-start | bytes 5111812
  40.3 14.0 %collective-permute-start.5 = (bf16[16,2,4,1664]{3,2,1,0:T(4,128)(2,1)S(1)}, bf16[16,2,4,1664]{3,2,1,0:T(4,128)(2,1)S(1)}, u32[]{:S(2)}, u32[]{:S(2)}) collective-permute-start(bf16[16,2,4,1664]{3,2,1,0:T(4,128)(2,1)S(1)} %get-tuple-element.106), channel_id=1, source_target_pairs={{0,2},{1,3},{2,4},{3,5},{4,6},{5,7},{6,0},{7,1},{8,10},{9,11},{10,... | collective-permute-start | bytes 1277960 | tf_op jit(solution)/shard_map/ppermute | solution.py:248
  41.8 12.8 %collective-permute-start.2 = (bf16[16,2,4,1664]{3,2,1,0:T(4,128)(2,1)S(1)}, bf16[16,2,4,1664]{3,2,1,0:T(4,128)(2,1)S(1)}, u32[]{:S(2)}, u32[]{:S(2)}) collective-permute-start(bf16[16,2,4,1664]{3,2,1,0:T(4,128)(2,1)S(1)} %get-tuple-element.107), channel_id=1, source_target_pairs={{0,6},{1,7},{2,0},{3,1},{4,2},{5,3},{6,4},{7,5},{8,14},{9,15},{10,... | collective-permute-start | bytes 1277960 | tf_op jit(solution)/shard_map/ppermute | solution.py:248
  43.6 20.1 %collective-permute-start.3 = (bf16[16,2,4,1664]{3,2,1,0:T(4,128)(2,1)S(1)}, bf16[16,2,4,1664]{3,2,1,0:T(4,128)(2,1)S(1)}, u32[]{:S(2)}, u32[]{:S(2)}) collective-permute-start(bf16[16,2,4,1664]{3,2,1,0:T(4,128)(2,1)S(1)} %get-tuple-element.106), channel_id=1, source_target_pairs={{0,6},{1,7},{2,0},{3,1},{4,2},{5,3},{6,4},{7,5},{8,14},{9,15},{10,... | collective-permute-start | bytes 1277960 | tf_op jit(solution)/shard_map/ppermute | solution.py:248
  45.1 18.6 %collective-permute-start.4 = (bf16[16,2,4,1664]{3,2,1,0:T(4,128)(2,1)S(1)}, bf16[16,2,4,1664]{3,2,1,0:T(4,128)(2,1)S(1)}, u32[]{:S(2)}, u32[]{:S(2)}) collective-permute-start(bf16[16,2,4,1664]{3,2,1,0:T(4,128)(2,1)S(1)} %get-tuple-element.107), channel_id=1, source_target_pairs={{0,2},{1,3},{2,4},{3,5},{4,6},{5,7},{6,0},{7,1},{8,10},{9,11},{10,... | collective-permute-start | bytes 1277960 | tf_op jit(solution)/shard_map/ppermute | solution.py:248
  54.3 18.3 %collective-permute-start.7 = (bf16[16,2,4,1664]{3,2,1,0:T(4,128)(2,1)S(1)}, bf16[16,2,4,1664]{3,2,1,0:T(4,128)(2,1)S(1)}, u32[]{:S(2)}, u32[]{:S(2)}) collective-permute-start(bf16[16,2,4,1664]{3,2,1,0:T(4,128)(2,1)S(1)} %collective-permute-done.5.refs_3_), channel_id=1, source_target_pairs={{0,2},{1,3},{2,4},{3,5},{4,6},{5,7},{6,0},{7,1},{8,10},{9,11},{10,... | collective-permute-start | bytes 1277960 | tf_op jit(solution)/shard_map/ppermute | solution.py:248
  54.6 18.3 %collective-permute-start.6 = (bf16[16,2,4,1664]{3,2,1,0:T(4,128)(2,1)S(1)}, bf16[16,2,4,1664]{3,2,1,0:T(4,128)(2,1)S(1)}, u32[]{:S(2)}, u32[]{:S(2)}) collective-permute-start(bf16[16,2,4,1664]{3,2,1,0:T(4,128)(2,1)S(1)} %collective-permute-done.2.refs_0_), channel_id=1, source_target_pairs={{0,6},{1,7},{2,0},{3,1},{4,2},{5,3},{6,4},{7,5},{8,14},{9,15},{10,... | collective-permute-start | bytes 1277960 | tf_op jit(solution)/shard_map/ppermute | solution.py:248
  68.7 14.0 %collective-permute-start.10 = (bf16[16,2,4,1664]{3,2,1,0:T(4,128)(2,1)S(1)}, bf16[16,2,4,1664]{3,2,1,0:T(4,128)(2,1)S(1)}, u32[]{:S(2)}, u32[]{:S(2)}) collective-permute-start(bf16[16,2,4,1664]{3,2,1,0:T(4,128)(2,1)S(1)} %get-tuple-element.67), channel_id=1, source_target_pairs={{0,2},{1,3},{2,4},{3,5},{4,6},{5,7},{6,0},{7,1},{8,10},{9,11},{10,... | collective-permute-start | bytes 1277960 | tf_op jit(solution)/shard_map/ppermute | solution.py:248
  70.3 12.7 %collective-permute-start.11 = (bf16[16,2,4,1664]{3,2,1,0:T(4,128)(2,1)S(1)}, bf16[16,2,4,1664]{3,2,1,0:T(4,128)(2,1)S(1)}, u32[]{:S(2)}, u32[]{:S(2)}) collective-permute-start(bf16[16,2,4,1664]{3,2,1,0:T(4,128)(2,1)S(1)} %get-tuple-element.68), channel_id=1, source_target_pairs={{0,6},{1,7},{2,0},{3,1},{4,2},{5,3},{6,4},{7,5},{8,14},{9,15},{10,... | collective-permute-start | bytes 1277960 | tf_op jit(solution)/shard_map/ppermute | solution.py:248
  76.9 11.4 %collective-permute-start.8 = (bf16[16,2,4,1664]{3,2,1,0:T(4,128)(2,1)S(1)}, bf16[16,2,4,1664]{3,2,1,0:T(4,128)(2,1)S(1)}, u32[]{:S(2)}, u32[]{:S(2)}) collective-permute-start(bf16[16,2,4,1664]{3,2,1,0:T(4,128)(2,1)S(1)} %get-tuple-element.71), channel_id=1, source_target_pairs={{0,2},{1,3},{2,4},{3,5},{4,6},{5,7},{6,0},{7,1},{8,10},{9,11},{10,... | collective-permute-start | bytes 1277960 | tf_op jit(solution)/shard_map/ppermute | solution.py:248
  78.5 10.1 %collective-permute-start.9 = (bf16[16,2,4,1664]{3,2,1,0:T(4,128)(2,1)S(1)}, bf16[16,2,4,1664]{3,2,1,0:T(4,128)(2,1)S(1)}, u32[]{:S(2)}, u32[]{:S(2)}) collective-permute-start(bf16[16,2,4,1664]{3,2,1,0:T(4,128)(2,1)S(1)} %get-tuple-element.73), channel_id=1, source_target_pairs={{0,6},{1,7},{2,0},{3,1},{4,2},{5,3},{6,4},{7,5},{8,14},{9,15},{10,... | collective-permute-start | bytes 1277960 | tf_op jit(solution)/shard_map/ppermute | solution.py:248
  88.8 9.4 %collective-permute-start.12 = (bf16[16,2,4,1664]{3,2,1,0:T(4,128)(2,1)S(1)}, bf16[16,2,4,1664]{3,2,1,0:T(4,128)(2,1)S(1)}, u32[]{:S(2)}, u32[]{:S(2)}) collective-permute-start(bf16[16,2,4,1664]{3,2,1,0:T(4,128)(2,1)S(1)} %add_convert_fusion.1), channel_id=1, source_target_pairs={{0,2},{1,3},{2,4},{3,5},{4,6},{5,7},{6,0},{7,1},{8,10},{9,11},{10,... | collective-permute-start | bytes 1277960 | tf_op jit(solution)/shard_map/ppermute | solution.py:248
  90.1 8.1 %collective-permute-start.13 = (bf16[16,2,4,1664]{3,2,1,0:T(4,128)(2,1)S(1)}, bf16[16,2,4,1664]{3,2,1,0:T(4,128)(2,1)S(1)}, u32[]{:S(2)}, u32[]{:S(2)}) collective-permute-start(bf16[16,2,4,1664]{3,2,1,0:T(4,128)(2,1)S(1)} %add_convert_fusion), channel_id=1, source_target_pairs={{0,6},{1,7},{2,0},{3,1},{4,2},{5,3},{6,4},{7,5},{8,14},{9,15},{10,... | collective-permute-start | bytes 1277960 | tf_op jit(solution)/shard_map/ppermute | solution.py:248
  92.1 14.4 %collective-permute-start.14 = (bf16[1664,512]{1,0:T(8,128)(2,1)}, bf16[1664,512]{1,0:T(8,128)(2,1)S(1)}, u32[]{:S(2)}, u32[]{:S(2)}) collective-permute-start(bf16[1664,512]{1,0:T(8,128)(2,1)} %get-tuple-element.98), channel_id=1, source_target_pairs={{0,1},{1,0},{2,3},{3,2},{4,5},{5,4},{6,7},{7,6},{8,9},{9,8},{10,11... | collective-permute-start | bytes 5111816 | tf_op jit(solution)/shard_map/ppermute | solution.py:248
  92.1 15.6 %collective-permute-start.15 = (bf16[512,1664]{1,0:T(8,128)(2,1)}, bf16[512,1664]{1,0:T(8,128)(2,1)}, u32[]{:S(2)}, u32[]{:S(2)}) collective-permute-start(bf16[512,1664]{1,0:T(8,128)(2,1)} %get-tuple-element.99), channel_id=1, source_target_pairs={{0,1},{1,0},{2,3},{3,2},{4,5},{5,4},{6,7},{7,6},{8,9},{9,8},{10,11... | collective-permute-start | bytes 5111816 | tf_op jit(solution)/shard_map/ppermute | solution.py:248
  99.7 27.6 %all-to-all-start.1 = ((bf16[32,2,4,1664]{3,2,1,0:T(4,128)(2,1)}), bf16[32,2,4,1664]{3,2,1,0:T(4,128)(2,1)S(1)}, u32[]{:S(2)}, u32[]{:S(2)}) async-start(bf16[32,2,4,1664]{3,2,1,0:T(4,128)(2,1)} %home_sum.1), calls=%async_computation.1 | async-start | bytes 1703936 | tf_op jit(solution)/shard_map/all_to_all | solution.py:251
  106.6 1.2 copy-start.4
  107.7 1.5 %copy-start.5 = (bf16[1664,512]{1,0:T(8,128)(2,1)S(1)}, bf16[1664,512]{1,0:T(8,128)(2,1)}, u32[]{:S(2)}) copy-start(bf16[1664,512]{1,0:T(8,128)(2,1)} %copy-done.4) | copy-start | bytes 5111812
  109.2 18.1 %copy-start.2 = (bf16[257,1664]{1,0:T(8,128)(2,1)S(1)}, bf16[257,1664]{1,0:T(8,128)(2,1)}, u32[]{:S(2)}) copy-start(bf16[257,1664]{1,0:T(8,128)(2,1)} %refs_4_.1) | copy-start | bytes 2565892
  109.2 18.1 %copy-start.3 = (bf16[257,1664]{1,0:T(8,128)(2,1)S(1)}, bf16[257,1664]{1,0:T(8,128)(2,1)}, u32[]{:S(2)}) copy-start(bf16[257,1664]{1,0:T(8,128)(2,1)} %refs_2_.1) | copy-start | bytes 2565892
  109.2 18.1 %copy-start.6 = (f32[1664]{0:T(1024)S(1)}, f32[1664]{0:T(1024)}, u32[]{:S(2)}) copy-start(f32[1664]{0:T(1024)} %refs_3_.1) | copy-start | bytes 19972
  109.2 18.1 %copy-start.7 = (f32[257,2]{0,1:T(2,128)S(1)}, f32[257,2]{0,1:T(2,128)}, u32[]{:S(2)}) copy-start(f32[257,2]{0,1:T(2,128)} %param.13) | copy-start | bytes 6172
